TPU v7x, 128 devices: a whole 4x4x4 slice. The times are simulated.
128 devices in a mesh: grp: 16 (over x, z), pr: 4 (over y), pc: 2 (over core).
Axes of the slice: x: 4, y: 4, z: 4, core: 2. Of those that a mesh axis runs over, the one named last changes fastest.
Arguments:
- pair_map: bfloat16 [1280, 1280, 128], P(('pr', 'pc'), 'grp'), may hold values from -6 to 6
- pair_mask: int32 [1280, 1280], P(('pr', 'pc'), 'grp'), may hold values 0 or 1
- input_gain: float32 [128], replicated, may hold values from 0.5 to 1.5
- input_bias: float32 [128], replicated, may hold values from -3 to 3
- input_weights: bfloat16 [128, 640], replicated, may hold values from -0.5 to 0.5
- output_gain: float32 [128], replicated, may hold values from 0.5 to 1.5
- output_bias: float32 [128], replicated, may hold values from -3 to 3
- output_weight: bfloat16 [128, 128], replicated, may hold values from -0.5 to 0.5
Outputs:
- update: bfloat16 [1280, 1280, 128], P(('pr', 'pc'), 'grp')
All inputs are finite; a program needn't handle non-finite values. No bound on the sum of `pair_mask` on one device may be relied on, other than what follows from the above.
Results may differ from a plain program's by a relative error of at most 0.0059.
Values may be sent and summed in bfloat16 or wider, within the bound.
A program may use at most 128 MiB of HBM per device.

v0:
```python
import jax
import jax.numpy as jnp
from jax import lax
from jax.sharding import PartitionSpec as P

epsilon = 1e-05


def layer_norm(values, scaling, offset, along):
    center = jnp.mean(values, axis=along, keepdims=True)
    shifted = values - center
    spread = jnp.mean(shifted * shifted, axis=along, keepdims=True)
    return shifted * lax.rsqrt(spread + epsilon) * scaling + offset


def gated_side(normed, weights, masking, value_start, channels):
    value_part = jnp.einsum(
        "rkc,cd->drk",
        normed,
        weights[:, value_start : value_start + channels],
        preferred_element_type=jnp.float32,
    )
    gate_part = jnp.einsum(
        "rkc,cd->drk",
        normed,
        weights[:, value_start + channels : value_start + 2 * channels],
        preferred_element_type=jnp.float32,
    )
    return (masking * jax.nn.sigmoid(gate_part) * value_part).astype(jnp.bfloat16)


def per_device(
    pair_map,
    pair_mask,
    input_gain,
    input_bias,
    input_weights,
    output_gain,
    output_bias,
    output_weight,
):
    channels = pair_map.shape[2]
    normed = layer_norm(pair_map.astype(jnp.float32), input_gain, input_bias, -1).astype(
        jnp.bfloat16
    )
    masking = pair_mask.astype(jnp.float32)[None]
    left_side = gated_side(normed, input_weights, masking, 0, channels)
    right_side = gated_side(normed, input_weights, masking, 2 * channels, channels)
    gate_out = jax.nn.sigmoid(
        jnp.einsum(
            "rkc,cd->rkd",
            normed,
            input_weights[:, 4 * channels :],
            preferred_element_type=jnp.float32,
        )
    )
    left_group, right_group = (
        lax.all_to_all(left_side, "grp", split_axis=0, concat_axis=2, tiled=True),
        lax.all_to_all(right_side, "grp", split_axis=0, concat_axis=2, tiled=True),
    )
    triangle = jnp.einsum(
        "cik,cjk->cij",
        left_group,
        lax.all_gather(right_group, ("pr", "pc"), axis=1, tiled=True),
        preferred_element_type=jnp.float32,
    ).astype(jnp.bfloat16)
    regrouped = lax.all_to_all(triangle, "grp", split_axis=2, concat_axis=0, tiled=True)
    settled = layer_norm(
        regrouped.astype(jnp.float32), output_gain[:, None, None], output_bias[:, None, None], 0
    ).astype(jnp.bfloat16)
    mixed = jnp.einsum("crk,cd->rkd", settled, output_weight, preferred_element_type=jnp.float32)
    return (gate_out * mixed).astype(jnp.bfloat16)


def solution(mesh):
    return jax.shard_map(
        per_device,
        mesh=mesh,
        in_specs=(
            P(("pr", "pc"), "grp", None),
            P(("pr", "pc"), "grp"),
            P(),
            P(),
            P(),
            P(),
            P(),
            P(),
        ),
        out_specs=P(("pr", "pc"), "grp", None),
        check_vma=False,
    )
```

profile of v0, /device:TPU:1, one launch (start us, length us, event | category | flops | bytes accessed | tf_op | source)
XLA Modules:
  0.0 379.6 jit_solution(16495077612412603429)
XLA Ops:
  7.6 3.4 convert_reduce_fusion
  11.0 5.9 %fusion.8 = f32[160,80]{1,0:T(8,128)S(1)} fusion(bf16[160,80,128]{2,1,0:T(8,128)(2,1)} %param.8, f32[160,80]{1,0:T(8,128)S(1)} %broadcast_multiply_fusion.1), kind=kLoop, calls=%fused_computation.13 | loop fusion | flops 6540800 | bytes 3379200 | tf_op jit(solution)/shard_map/reduce_sum | solution.py:12
  17.0 4.3 %fusion.18 = f32[160,80,128]{2,1,0:T(8,128)S(1)} fusion(bf16[128,640]{1,0:T(8,128)(2,1)} %param.12, bf16[160,80,128]{2,1,0:T(8,128)(2,1)S(1)} %copy-done.2, f32[128]{0:T(128)S(1)} %copy-done.4, f32[128]{0:T(128)S(1)} %copy-done.7, f32[160,80]{1,0:T(8,128)S(1)} %add_rsqrt_fusion.1, f32[160,80]{1,0:T(8,128)S(1)} %broadcast_multiply_fusion.1), kind=kOutput, calls=%fused_computation.31 | convolution fusion | flops 429260800 | bytes 9966592 | tf_op jit(solution)/shard_map/rkc,cd->drk/dot_general | solution.py:23
  21.4 8.2 %fusion.15 = bf16[128,160,80]{0,2,1:T(8,128)(2,1)} fusion(f32[160,80,128]{2,1,0:T(8,128)S(1)} %fusion.18, f32[160,80]{1,0:T(8,128)S(1)} %convert_element_type.44, bf16[128,640]{1,0:T(8,128)(2,1)} %param.12, bf16[160,80,128]{2,1,0:T(8,128)(2,1)S(1)} %copy-done.2, f32[128]{0:T(128)S(1)} %copy-done.4, f32[128]{0:T(128)S(1)} %copy-done.7, ...), kind=kOutput, calls=%fused_computation.24 | convolution fusion | flops 439091200 | bytes 13294592 | tf_op jit(solution)/shard_map/rkc,cd->drk/dot_general | solution.py:17
  29.6 7.4 %copy.20 = bf16[128,160,80]{2,1,0:T(8,128)(2,1)} copy(bf16[128,160,80]{0,2,1:T(8,128)(2,1)} %fusion.15) | data formatting | bytes 6553600 | tf_op jit(solution)/shard_map/convert_element_type | solution.py:29
  37.1 69.0 %all_to_all.45 = bf16[128,160,80]{2,1,0:T(8,128)(2,1)S(1)} all-to-all(bf16[128,160,80]{2,1,0:T(8,128)(2,1)} %copy.20), channel_id=1, replica_groups=mesh['grp'=16,'pr'=4,'pc'=2] {'grp'}, dimensions={0} | all-to-all | bytes 6553600 | tf_op jit(solution)/shard_map/all_to_all | solution.py:59
  106.1 5.7 %copy.21 = bf16[8,160,16,80]{3,2,1,0:T(8,128)(2,1)} copy(bf16[8,160,16,80]{3,1,0,2:T(8,128)(2,1)S(1)} %bitcast.54) | data formatting | bytes 6553600 | tf_op jit(solution)/shard_map/all_to_all | solution.py:59
  111.7 9.1 %all_to_all.40 = bf16[8,160,1280]{2,1,0:T(8,128)(2,1)} reshape(bf16[8,160,16,80]{3,2,1,0:T(8,128)(2,1)} %copy.21) | data formatting | bytes 6553600 | tf_op jit(solution)/shard_map/all_to_all | solution.py:59
  120.9 4.4 %fusion.21 = f32[160,80,128]{2,1,0:T(8,128)S(1)} fusion(bf16[128,640]{1,0:T(8,128)(2,1)} %param.12, bf16[160,80,128]{2,1,0:T(8,128)(2,1)S(1)} %copy-done.2, f32[128]{0:T(128)} %param.11, f32[128]{0:T(128)} %param.10, f32[160,80]{1,0:T(8,128)S(1)} %add_rsqrt_fusion.1, f32[160,80]{1,0:T(8,128)S(1)} %broadcast_multiply_fusion.1), kind=kOutput, calls=%fused_computation.34 | convolution fusion | flops 429260800 | bytes 9966592 | tf_op jit(solution)/shard_map/rkc,cd->drk/dot_general | solution.py:23
  125.3 8.3 %fusion.14 = bf16[128,160,80]{0,2,1:T(8,128)(2,1)} fusion(f32[160,80,128]{2,1,0:T(8,128)S(1)} %fusion.21, f32[160,80]{1,0:T(8,128)S(1)} %convert_element_type.44, bf16[128,640]{1,0:T(8,128)(2,1)} %param.12, bf16[160,80,128]{2,1,0:T(8,128)(2,1)S(1)} %copy-done.2, f32[128]{0:T(128)S(1)} %copy-done.5, f32[128]{0:T(128)S(1)} %copy-done.8, ...), kind=kOutput, calls=%fused_computation.23 | convolution fusion | flops 439091200 | bytes 13294592 | tf_op jit(solution)/shard_map/rkc,cd->drk/dot_general | solution.py:17
  133.6 7.7 %copy.18 = bf16[128,160,80]{2,1,0:T(8,128)(2,1)} copy(bf16[128,160,80]{0,2,1:T(8,128)(2,1)} %fusion.14) | data formatting | bytes 6553600 | tf_op jit(solution)/shard_map/convert_element_type | solution.py:29
  141.3 64.5 %all_to_all.46 = bf16[128,160,80]{2,1,0:T(8,128)(2,1)S(1)} all-to-all(bf16[128,160,80]{2,1,0:T(8,128)(2,1)} %copy.18), channel_id=1, replica_groups=mesh['grp'=16,'pr'=4,'pc'=2] {'grp'}, dimensions={0} | all-to-all | bytes 6553600 | tf_op jit(solution)/shard_map/all_to_all | solution.py:58
  205.8 5.8 %copy.19 = bf16[8,160,16,80]{3,2,1,0:T(8,128)(2,1)} copy(bf16[8,160,16,80]{3,1,0,2:T(8,128)(2,1)S(1)} %bitcast.55) | data formatting | bytes 6553600 | tf_op jit(solution)/shard_map/all_to_all | solution.py:58
  211.5 8.0 %all_to_all.36 = bf16[8,160,1280]{2,1,0:T(8,128)(2,1)S(1)} reshape(bf16[8,160,16,80]{3,2,1,0:T(8,128)(2,1)} %copy.19) | data formatting | bytes 6553600 | tf_op jit(solution)/shard_map/all_to_all | solution.py:58
  219.5 27.2 %all-gather.2.cloned.1.call-done = bf16[8,1280,1280]{2,1,0:T(8,128)(2,1)} async-done(((bf16[8,160,1280]{2,1,0:T(8,128)(2,1)}), bf16[8,1280,1280]{2,1,0:T(8,128)(2,1)}) %all-gather.2.cloned.1.call-update) | async-done | bytes 26214416 | tf_op jit(solution)/shard_map/all_gather | solution.py:64
  246.7 14.7 %convolution_convert_fusion = bf16[8,160,1280]{2,1,0:T(8,128)(2,1)} fusion(bf16[8,160,1280]{2,1,0:T(8,128)(2,1)S(1)} %all_to_all.36, bf16[8,1280,1280]{2,1,0:T(8,128)(2,1)} %all-gather.2.cloned.1.call-done), kind=kOutput, calls=%fused_computation.22 | convolution fusion | flops 4195942400 | bytes 32768000 | tf_op jit(solution)/shard_map/cik,cjk->cij/dot_general | solution.py:61
  261.4 8.7 %copy.22 = bf16[8,160,1280]{1,0,2:T(8,128)(2,1)} copy(bf16[8,160,1280]{2,1,0:T(8,128)(2,1)} %convolution_convert_fusion) | data formatting | bytes 6553600 | tf_op jit(solution)/shard_map/convert_element_type | solution.py:66
  270.1 67.6 %all_to_all.47 = bf16[8,160,1280]{1,0,2:T(8,128)(2,1)} all-to-all(bf16[8,160,1280]{1,0,2:T(8,128)(2,1)} %copy.22), channel_id=1, replica_groups=mesh['grp'=16,'pr'=4,'pc'=2] {'grp'}, dimensions={2} | all-to-all | bytes 6553600 | tf_op jit(solution)/shard_map/all_to_all | solution.py:67
  337.7 9.8 %copy.23 = f32[8,160,16,80]{3,1,0,2:T(8,128)} copy(bf16[8,160,16,80]{1,0,3,2:T(8,128)(2,1)} %bitcast.56) | data formatting | bytes 9830400 | tf_op jit(solution)/shard_map/convert_element_type | solution.py:69
  347.5 4.9 %bitcast_reduce_fusion = f32[160,80]{1,0:T(8,128)S(1)} fusion(f32[8,160,16,80]{3,1,0,2:T(8,128)} %copy.23), kind=kLoop, calls=%fused_computation.5 | loop fusion | flops 1625600 | bytes 6604800 | tf_op jit(solution)/shard_map/reduce_sum | solution.py:10
  352.4 2.0 copy-done.1
  355.9 4.2 %fusion.3 = bf16[128,160,80]{2,1,0:T(8,128)(2,1)} fusion(f32[8,160,16,80]{3,1,0,2:T(8,128)S(1)} %copy-done.1, f32[128]{0:T(128)S(1)} %copy-done.10, f32[128]{0:T(128)S(1)} %copy-done.11, f32[160,80]{1,0:T(8,128)S(1)} %add_rsqrt_fusion, f32[160,80]{1,0:T(8,128)S(1)} %broadcast_multiply_fusion), kind=kLoop, calls=%fused_computation.4 | loop fusion | flops 8192000 | bytes 9933824 | tf_op jit(solution)/shard_map/convert_element_type | solution.py:70
  360.1 4.9 %fusion.12 = f32[160,80,128]{2,1,0:T(8,128)S(1)} fusion(bf16[128,160,80]{2,1,0:T(8,128)(2,1)} %fusion.3, bf16[128,128]{1,0:T(8,128)(2,1)S(1)} %copy-done), kind=kOutput, calls=%fused_computation.20 | convolution fusion | flops 419430400 | bytes 9863168 | tf_op jit(solution)/shard_map/crk,cd->rkd/dot_general | solution.py:71
  365.0 7.7 %multiply_convert_fusion.2 = bf16[160,80,128]{2,1,0:T(8,128)(2,1)} fusion(f32[160,80,128]{2,1,0:T(8,128)S(1)} %fusion.12, bf16[128,640]{1,0:T(8,128)(2,1)} %param.12, bf16[160,80,128]{2,1,0:T(8,128)(2,1)S(1)} %copy-done.3, f32[128]{0:T(128)S(1)} %copy-done.6, f32[128]{0:T(128)S(1)} %copy-done.9, f32[160,80]{1,0:T(8,128)S(1)} %add_rsqrt_fusion.1, ...), kind=kOutput, calls=%fused_computation.19 | convolution fusion | flops 437452800 | bytes 13243392 | tf_op jit(solution)/shard_map/rkc,cd->rkd/dot_general | solution.py:50
  (31 shorter events, 2.6 us)
Async XLA Ops:
  6.5 353.6 %copy-start = (bf16[128,128]{1,0:T(8,128)(2,1)S(1)}, bf16[128,128]{1,0:T(8,128)(2,1)}, u32[]{:S(2)}) copy-start(bf16[128,128]{1,0:T(8,128)(2,1)} %param.15) | copy-start | bytes 98308
  6.5 10.5 %copy-start.2 = (bf16[160,80,128]{2,1,0:T(8,128)(2,1)S(1)}, bf16[160,80,128]{2,1,0:T(8,128)(2,1)}, u32[]{:S(2)}) copy-start(bf16[160,80,128]{2,1,0:T(8,128)(2,1)} %param.8) | copy-start | bytes 9830404
  6.5 240.2 %all-gather.2.cloned.1.call-start = ((), (), s32[]{:S(2)}) async-start(), calls=%async_computation.3 | async-start | bytes 29491200 | tf_op jit(solution)/shard_map/all_gather | solution.py:64
  6.5 10.5 %copy-start.4 = (f32[128]{0:T(128)S(1)}, f32[128]{0:T(128)}, u32[]{:S(2)}) copy-start(f32[128]{0:T(128)} %param.11) | copy-start | bytes 1540
  6.5 10.5 %copy-start.7 = (f32[128]{0:T(128)S(1)}, f32[128]{0:T(128)}, u32[]{:S(2)}) copy-start(f32[128]{0:T(128)} %param.10) | copy-start | bytes 1540
  120.9 4.4 %copy-start.5 = (f32[128]{0:T(128)S(1)}, f32[128]{0:T(128)}, u32[]{:S(2)}) copy-start(f32[128]{0:T(128)} %param.11) | copy-start | bytes 1540
  120.9 4.4 %copy-start.8 = (f32[128]{0:T(128)S(1)}, f32[128]{0:T(128)}, u32[]{:S(2)}) copy-start(f32[128]{0:T(128)} %param.10) | copy-start | bytes 1540
  347.5 7.0 %copy-start.1 = (f32[8,160,16,80]{3,1,0,2:T(8,128)S(1)}, f32[8,160,16,80]{3,1,0,2:T(8,128)}, u32[]{:S(2)}) copy-start(f32[8,160,16,80]{3,1,0,2:T(8,128)} %copy.23) | copy-start | bytes 19660804
  352.4 3.5 copy-start.10
  352.4 3.5 copy-start.11
  360.1 4.9 %copy-start.3 = (bf16[160,80,128]{2,1,0:T(8,128)(2,1)S(1)}, bf16[160,80,128]{2,1,0:T(8,128)(2,1)}, u32[]{:S(2)}) copy-start(bf16[160,80,128]{2,1,0:T(8,128)(2,1)} %param.8) | copy-start | bytes 9830404
  360.1 4.9 %copy-start.6 = (f32[128]{0:T(128)S(1)}, f32[128]{0:T(128)}, u32[]{:S(2)}) copy-start(f32[128]{0:T(128)} %param.11) | copy-start | bytes 1540
  360.1 4.9 %copy-start.9 = (f32[128]{0:T(128)S(1)}, f32[128]{0:T(128)}, u32[]{:S(2)}) copy-start(f32[128]{0:T(128)} %param.10) | copy-start | bytes 1540
Sparse Core Ops, SparseCore 0:
  121.0 125.6 all-gather.1
where the time goes:
time: 382 us; the launch traced here: 380 us
  blocking collectives  201 us (53%)
  local copies, waits for them, and re-layouts  64.2 us (17%)
  matrix products  52.6 us (14%)
  waiting for transfers between devices  27.2 us (7%)
  other arithmetic  20.9 us (5%)
  between operations  13.6 us (4%)
    all_to_all x1, blocking collectives, per_device(): lax.all_to_all(right_side, 'grp', split_axis=0, concat_axis=2, tiled=True)  69 us
    all_to_all x1, blocking collectives, per_device(): lax.all_to_all(triangle, 'grp', split_axis=2, concat_axis=0, tiled=True)  67.6 us
    all_to_all x1, blocking collectives, per_device(): lax.all_to_all(left_side, 'grp', split_axis=0, concat_axis=2, tiled=True)  64.5 us
    all_gather x1, waiting for transfers between devices, per_device(): lax.all_gather(right_group, ('pr', 'pc'), axis=1, tiled=True)  27.2 us
    dot_general x2, matrix products, gated_side(): jnp.einsum('rkc,cd->drk', normed, weights[:, value_start:value_start + ch...  16.5 us
    convert_element_type x2, local copies, waits for them, and re-layouts, gated_side(): (masking * jax.nn.sigmoid(gate_part) * value_part).astype(jnp.bfloat16)  15.1 us
    all_to_all x2, local copies, waits for them, and re-layouts, per_device(): lax.all_to_all(right_side, 'grp', split_axis=0, concat_axis=2, tiled=True)  14.8 us
    dot_general x1, matrix products, per_device(): jnp.einsum('cik,cjk->cij', left_group, lax.all_gather(right_group, ('pr',...  14.7 us
  transfers between devices with their start and end apart: 1, of which 1 were waited for; matrix products, arithmetic and copies ran while one was open for 7% of the time, Pallas kernels for 0%

commit v1 on v0

v1 whole, which is shorter than its diff:
```python
import jax
import jax.numpy as jnp
from jax import lax
from jax.experimental import pallas as pl
from jax.experimental.pallas import tpu as pltpu
from jax.sharding import PartitionSpec as P

MESH = pl.DeviceIdType.MESH
F32 = jnp.float32
BF16 = jnp.bfloat16
epsilon = 1e-05

I = 160
K = 80
C = 128
G = 16
A = 8
ROWS = 104
N = 1280


def mod(value, by):
    return lax.rem(value, by)


def kernel(
    x_ref,
    mask_ref,
    gain_ref,
    bias_ref,
    proj_ref,
    gatew_ref,
    ogain_ref,
    obias_ref,
    ow_ref,
    o_ref,
    normed,
    gates,
    swap,
    out_l,
    out_r,
    in_l,
    in_r,
    rest_l,
    rest_r,
    right_t,
    out_t,
    in_t,
    send_sem,
    recv_sem,
):
    g = lax.axis_index("grp")
    y = lax.axis_index("pr")
    core = lax.axis_index("pc")
    x, z = g // 4, mod(g, 4)
    a = y * 2 + core
    quarter = mod(a, 4)
    mine = g * A + a

    def partner(step):
        v = mod(step * 11, 128)
        px = mod(x + mod(v, 4), 4)
        py = mod(y + mod(v // 4, 4), 4)
        pcore = mod(core + mod(v // 16, 2), 2)
        pz = mod(z + v // 32, 4)
        return px * 4 + pz, py, pcore

    barrier = pltpu.get_barrier_semaphore()

    def greet(step, carry):
        pg, py, pcore = partner(step)
        pl.semaphore_signal(
            barrier, inc=1, device_id={"grp": pg, "pr": py, "pc": pcore}, device_id_type=MESH
        )
        return carry

    lax.fori_loop(1, 128, greet, 0)

    lane_group = lax.broadcasted_iota(jnp.int32, (8, 128), 1) // 32

    def by_group(parts):
        group = lax.broadcasted_iota(jnp.int32, parts[0].shape, 1) // 32
        return jnp.where(
            group == 0, parts[0], jnp.where(group == 1, parts[1], jnp.where(group == 2, parts[2], parts[3]))
        )

    def token(s, r, low):
        n = mod(quarter - s + 4, 4)
        return n * 16 + r if low else 64 + n * 4 + r

    def normalize(k, carry):
        rows = x_ref[k].astype(F32)
        center = jnp.mean(rows, axis=-1, keepdims=True)
        shifted = rows - center
        spread = jnp.mean(shifted * shifted, axis=-1, keepdims=True)
        normed[k] = (
            shifted * lax.rsqrt(spread + epsilon) * gain_ref[...] + bias_ref[...]
        ).astype(BF16)
        return carry

    lax.fori_loop(0, K, normalize, 0)

    def gated(tokens, weights, mask_rows):
        both = lax.dot_general(
            weights, tokens, (((1,), (1,)), ((), ())), preferred_element_type=F32
        )
        value, gate = both[:C], both[C:]
        return value * jax.nn.sigmoid(gate) * mask_rows

    def unswap(store, rows, at):
        def one(c, carry):
            store[c, pl.ds(at, rows), :] = swap[pl.ds(c, rows, stride=C), :].astype(BF16)
            return carry

        lax.fori_loop(0, C, one, 0, unroll=8)

    def rest_tokens(r, low):
        return jnp.concatenate(
            [normed[token(s, r, low), 128:, :] for s in range(4)], axis=0
        )

    def rest_mask(r, low):
        return by_group([mask_ref[1, pl.ds(token(s, r, low), 1), :] for s in range(4)])

    def project(first, store):
        weights = proj_ref[first : first + 2 * C, :]

        def block(b, carry):
            def pair(p, carry):
                k = b * 16 + p * 2
                tokens = normed[pl.ds(k, 2), 0:128, :].reshape(256, C)
                rows = mask_ref[0, pl.ds(k, 2), :]
                result = gated(
                    tokens, weights, jnp.concatenate([rows[0:1], rows[1:2]], axis=1)
                )
                swap[pl.ds(p * 256, C), :] = result[:, :128]
                swap[pl.ds(p * 256 + C, C), :] = result[:, 128:]
                return carry

            lax.fori_loop(0, 8, pair, 0)
            unswap(store, 16, pl.multiple_of(b * 16, 16))
            return carry

        lax.fori_loop(0, 5, block, 0)

        for low, pairs, rows, at in ((True, 8, 16, 80), (False, 2, 8, 96)):

            def rest(p, carry):
                r = p * 2
                tokens = jnp.concatenate([rest_tokens(r, low), rest_tokens(r + 1, low)], axis=0)
                result = gated(
                    tokens,
                    weights,
                    jnp.concatenate([rest_mask(r, low), rest_mask(r + 1, low)], axis=1),
                )
                swap[pl.ds(p * 256, C), :] = result[:, :128]
                swap[pl.ds(p * 256 + C, C), :] = result[:, 128:]
                return carry

            lax.fori_loop(0, pairs, rest, 0)
            unswap(store, rows, at)

    def send_side(source, target, which):
        def one(step, carry):
            pg, py, pcore = partner(step)
            pltpu.make_async_remote_copy(
                src_ref=source.at[pg * A + py * 2 + pcore],
                dst_ref=target.at[a, g],
                send_sem=send_sem.at[which],
                recv_sem=recv_sem.at[which],
                device_id={"grp": pg, "pr": py, "pc": pcore},
                device_id_type=MESH,
            ).start()
            return carry

        pltpu.make_async_copy(source.at[mine], target.at[a, g], recv_sem.at[which]).start()
        lax.fori_loop(1, 128, one, 0)

    def wait_all(buffer, semaphore):
        pltpu.make_async_copy(buffer, buffer, semaphore).wait()

    project(2 * C, out_r)
    pl.semaphore_wait(barrier, 127)
    send_side(out_r, in_r, 0)
    project(0, out_l)
    send_side(out_l, in_l, 1)

    def open_gate(p, carry):
        tokens = normed[pl.ds(p * 2, 2)].reshape(2 * I, C)
        gates[pl.ds(p * 2, 2)] = jax.nn.sigmoid(
            jnp.dot(tokens, gatew_ref[...], preferred_element_type=F32)
        ).reshape(2, I, C)
        return carry

    lax.fori_loop(0, K // 2, open_gate, 0)

    def spread_rest(arrived, rest):
        def one(step, carry):
            h, sg = step // G, mod(step, G)
            parts = [arrived[4 * h + t, sg, 80:96, :].astype(F32) for t in range(4)]
            tails = [arrived[4 * h + t, sg, 96:104, :].astype(F32) for t in range(4)]
            at = sg * K
            ends = []
            for n in range(4):
                rows = by_group([parts[(s + n) % 4] for s in range(4)])
                tail = by_group([tails[(s + n) % 4] for s in range(4)])
                if n:
                    rows = pltpu.roll(rows, 32 * n, 1)
                    tail = pltpu.roll(tail, 32 * n, 1)
                rest[h, pl.ds(pl.multiple_of(at + n * 16, 16), 16), :] = rows.astype(BF16)
                ends.append(tail)
            upper = lax.broadcasted_iota(jnp.int32, (8, 128), 0) < 4
            joined = jnp.concatenate(
                [
                    jnp.where(upper, ends[0], pltpu.roll(ends[1], 4, 0)),
                    jnp.where(upper, ends[2], pltpu.roll(ends[3], 4, 0)),
                ],
                axis=0,
            )
            rest[h, pl.ds(pl.multiple_of(at + 64, 16), 16), :] = joined.astype(BF16)
            return carry

        lax.fori_loop(0, 2 * G, one, 0)

    wait_all(in_r, recv_sem.at[0])
    spread_rest(in_r, rest_r)

    def turn_main(b, carry):
        tile = in_r[b, :, 0:K, :].reshape(N, 128)
        right_t[pl.ds(pl.multiple_of(b * I, 32), 128), :] = tile.T
        return carry

    lax.fori_loop(0, A, turn_main, 0)

    def turn_rest(h, carry):
        turned = rest_r[h].T
        for t in range(4):
            right_t[pl.ds(pl.multiple_of((4 * h + t) * I + 128, 32), 32), :] = turned[
                32 * t : 32 * t + 32
            ]
        return carry

    lax.fori_loop(0, 2, turn_rest, 0)

    wait_all(in_l, recv_sem.at[1])
    spread_rest(in_l, rest_l)

    def rest_product(m, carry):
        rows = right_t[pl.ds(pl.multiple_of(m * 320, 32), 320), :]
        columns = jnp.concatenate([rest_l[0], rest_l[1]], axis=1)
        product = jnp.dot(rows, columns, preferred_element_type=F32)
        for h in range(2):
            for sg in range(4):
                block = product[sg * K : (sg + 1) * K, h * 128 : (h + 1) * 128]
                mains, tails = [], []
                for n in range(4):
                    main = block[n * 16 : (n + 1) * 16]
                    tail = block[64 + 8 * (n // 2) : 72 + 8 * (n // 2)]
                    if n % 2:
                        tail = pltpu.roll(tail, 4, 0)
                    if n:
                        main = pltpu.roll(main, 128 - 32 * n, 1)
                        tail = pltpu.roll(tail, 128 - 32 * n, 1)
                    mains.append(main)
                    tails.append(tail)
                for t in range(4):
                    out_t[m * 4 + sg, 4 * h + t, 80:96, :] = by_group(
                        [mains[(t - s) % 4] for s in range(4)]
                    ).astype(BF16)
                    out_t[m * 4 + sg, 4 * h + t, 96:104, :] = by_group(
                        [tails[(t - s) % 4] for s in range(4)]
                    ).astype(BF16)
        return carry

    lax.fori_loop(0, 4, rest_product, 0)

    def main_product(step, carry):
        ty = mod(y + step, 4)

        def part(m, carry):
            rows = right_t[pl.ds(pl.multiple_of(m * 320, 32), 320), :]
            columns = jnp.concatenate(
                [in_l[2 * ty + i, :, 0:K, :].reshape(N, 128) for i in range(2)], axis=1
            )
            product = jnp.dot(rows, columns, preferred_element_type=F32).astype(BF16)
            for i in range(2):
                out_t[pl.ds(m * 4, 4), 2 * ty + i, 0:K, :] = product[
                    :, i * 128 : (i + 1) * 128
                ].reshape(4, K, 128)
            return carry

        lax.fori_loop(0, 4, part, 0)
        return carry

    lax.fori_loop(0, 4, main_product, 0)

    def send_back(step, carry):
        pg, py, pcore = partner(step)
        pltpu.make_async_remote_copy(
            src_ref=out_t.at[pg, py * 2 + pcore],
            dst_ref=in_t.at[mine],
            send_sem=send_sem.at[2],
            recv_sem=recv_sem.at[2],
            device_id={"grp": pg, "pr": py, "pc": pcore},
            device_id_type=MESH,
        ).start()
        return carry

    pltpu.make_async_copy(out_t.at[g, a], in_t.at[mine], recv_sem.at[2]).start()
    lax.fori_loop(1, 128, send_back, 0)

    wait_all(in_t, recv_sem.at[2])

    def settle(r, rows):
        values = swap[pl.ds(r, C, stride=rows), :]
        center = jnp.mean(values, axis=0, keepdims=True)
        shifted = values - center
        spread = jnp.mean(shifted * shifted, axis=0, keepdims=True)
        settled = (
            shifted * lax.rsqrt(spread + epsilon) * ogain_ref[...] + obias_ref[...]
        ).astype(BF16)
        return lax.dot_general(
            settled, ow_ref[...], (((0,), (0,)), ((), ())), preferred_element_type=F32
        )

    def widen(at, rows):
        def one(c, carry):
            swap[pl.ds(pl.multiple_of(c * rows, 8), rows), :] = in_t[c, pl.ds(at, rows), :].astype(F32)
            return carry

        lax.fori_loop(0, C, one, 0, unroll=8)

    def finish(b, carry):
        widen(pl.multiple_of(b * 16, 16), 16)

        def one(r, carry):
            j = b * 16 + r
            o_ref[j, 0:128, :] = (gates[j, 0:128, :] * settle(r, 16)).astype(BF16)
            return carry

        lax.fori_loop(0, 16, one, 0)
        return carry

    lax.fori_loop(0, 5, finish, 0)

    for low, count, rows, at in ((True, 16, 16, 80), (False, 4, 8, 96)):
        widen(at, rows)

        def one_rest(r, carry):
            mixed = settle(r, rows)
            for s in range(4):
                j = token(s, r, low)
                o_ref[j, 128:, :] = (
                    gates[j, 128:, :] * mixed[32 * s : 32 * s + 32]
                ).astype(BF16)
            return carry

        lax.fori_loop(0, count, one_rest, 0)

    for which, buffer in ((0, out_r), (1, out_l), (2, in_t)):
        sent = buffer.at[pl.ds(0, 127)]
        pltpu.make_async_copy(sent, sent, send_sem.at[which]).wait()


def per_device(
    pair_map,
    pair_mask,
    input_gain,
    input_bias,
    input_weights,
    output_gain,
    output_bias,
    output_weight,
):
    turned = jnp.transpose(pair_map, (1, 0, 2))
    mask = pair_mask.astype(F32).T
    masks = jnp.stack([mask[:, :128], jnp.tile(mask[:, 128:], (1, 4))])
    weights = input_weights[:, : 4 * C].T
    gate_weights = input_weights[:, 4 * C :]
    gains = jnp.broadcast_to(output_gain[:, None], (C, 128))
    offsets = jnp.broadcast_to(output_bias[:, None], (C, 128))
    vmem = pl.BlockSpec(memory_space=pltpu.VMEM)
    result = pl.pallas_call(
        kernel,
        out_shape=jax.ShapeDtypeStruct((K, I, C), BF16),
        in_specs=[vmem] * 9,
        out_specs=vmem,
        scratch_shapes=[
            pltpu.VMEM((K, I, C), BF16),
            pltpu.VMEM((K, I, C), F32),
            pltpu.VMEM((16 * C, 128), F32),
            pltpu.VMEM((C, ROWS, 128), BF16),
            pltpu.VMEM((C, ROWS, 128), BF16),
            pltpu.VMEM((A, G, ROWS, 128), BF16),
            pltpu.VMEM((A, G, ROWS, 128), BF16),
            pltpu.VMEM((2, N, 128), BF16),
            pltpu.VMEM((2, N, 128), BF16),
            pltpu.VMEM((N, N), BF16),
            pltpu.VMEM((G, A, ROWS, 128), BF16),
            pltpu.VMEM((C, ROWS, 128), BF16),
            pltpu.SemaphoreType.DMA((3,)),
            pltpu.SemaphoreType.DMA((3,)),
        ],
        compiler_params=pltpu.CompilerParams(
            collective_id=0, has_side_effects=True, vmem_limit_bytes=56 * 2**20
        ),
        cost_estimate=pl.CostEstimate(
            flops=6_500_000_000, bytes_accessed=16_000_000, transcendentals=5_000_000
        ),
    )(
        turned,
        masks,
        input_gain[None],
        input_bias[None],
        weights,
        gate_weights,
        gains,
        offsets,
        output_weight,
    )
    return jnp.transpose(result, (1, 0, 2))


def solution(mesh):
    return jax.shard_map(
        per_device,
        mesh=mesh,
        in_specs=(
            P(("pr", "pc"), "grp", None),
            P(("pr", "pc"), "grp"),
            P(),
            P(),
            P(),
            P(),
            P(),
            P(),
        ),
        out_specs=P(("pr", "pc"), "grp", None),
        check_vma=False,
    )
```

time: 382 us -> 216 us (0.57)
  blocking collectives: 201 us -> 0 us
  Pallas kernels: 0 us -> 199 us
  matrix products: 52.6 us -> 0 us
  local copies, waits for them, and re-layouts: 64.2 us -> 16.3 us
  waiting for transfers between devices: 27.2 us -> 0 us
  other arithmetic: 20.9 us -> 0.65 us
  between operations: 13.6 us -> 0.06 us
    all_to_all x3 -> x0, blocking collectives: 201 us -> none  [the longest x1 69 us: per_device(): lax.all_to_all(right_side, 'grp', split_axis=0, concat_axis=2, tiled=True)]
    pallas_call x0 -> x1, Pallas kernels: none -> 199 us  [per_device(): pl.pallas_call(kernel, out_shape=jax.ShapeDtypeStruct((K, I, C), BF16), i...]
    dot_general x7 -> x0, matrix products: 52.6 us -> none  [the longest x2 16.5 us: gated_side(): jnp.einsum('rkc,cd->drk', normed, weights[:, value_start:value_start + ch...]
    convert_element_type x4 -> x0, local copies, waits for them, and re-layouts: 33.6 us -> none  [the longest x2 15.1 us: gated_side(): (masking * jax.nn.sigmoid(gate_part) * value_part).astype(jnp.bfloat16)]
    all_to_all x4 -> x0, local copies, waits for them, and re-layouts: 28.5 us -> none  [the longest x2 14.8 us: per_device(): lax.all_to_all(right_side, 'grp', split_axis=0, concat_axis=2, tiled=True)]
    all_gather x1 -> x0, waiting for transfers between devices: 27.2 us -> none  [per_device(): lax.all_gather(right_group, ('pr', 'pc'), axis=1, tiled=True)]
    reduce_sum x4 -> x0, other arithmetic: 15.6 us -> none  [the longest x2 8.28 us: layer_norm(): center = jnp.mean(values, axis=along, keepdims=True)]
    convert_element_type x2 -> x0, other arithmetic: 5.24 us -> none  [the longest x1 4.19 us: per_device(): settled = layer_norm(regrouped.astype(jnp.float32), output_gain[:, None,...]
  transfers between devices with their start and end apart: 1 -> 0, of which waited for: 1 -> 0; matrix products, arithmetic and copies ran while one was open for 7% -> 0% of each run, Pallas kernels for 0% -> 0%
where the time goes in v1:
time: 216 us
  Pallas kernels  199 us (92%)
  local copies, waits for them, and re-layouts  16.3 us (8%)
    pallas_call x1, Pallas kernels, per_device(): pl.pallas_call(kernel, out_shape=jax.ShapeDtypeStruct((K, I, C), BF16), i...  199 us
    unnamed x3, local copies, waits for them, and re-layouts  6.19 us
    transpose x1, local copies, waits for them, and re-layouts, per_device(): return jnp.transpose(result, (1, 0, 2))  4.9 us

profile of v1, /device:TPU:1, one launch (start us, length us, event | category | flops | bytes accessed | tf_op | source)
XLA Modules:
  0.0 216.0 jit_solution(15119204572942909029)
XLA Ops:
  0.0 1.4 slice.15.gatew_ref
  1.4 1.4 broadcast_in_dim.20.ogain_ref
  2.7 1.4 broadcast_in_dim.21.obias_ref
  4.1 1.0 copy.14
  5.1 0.1 copy.15
  5.2 0.1 copy.16
  5.3 0.6 pad_maximum_fusion.mask_ref
  5.9 0.9 slice.14
  6.9 0.8 copy.19
  7.6 4.5 %copy.21 = bf16[160,80,128]{2,0,1:T(8,128)(2,1)} copy(bf16[160,80,128]{2,1,0:T(8,128)(2,1)} %param.8) | data formatting | bytes 6553600 | tf_op args[0]
  12.1 199.0 %shard_map.82 = bf16[80,160,128]{2,1,0:T(8,128)(2,1)} custom-call(bf16[80,160,128]{2,1,0:T(8,128)(2,1)} %bitcast.13, f32[2,80,128]{2,1,0:T(8,128)} %pad_maximum_fusion.mask_ref, f32[1,128]{1,0:T(1,128)} %bitcast.16, f32[1,128]{1,0:T(1,128)} %bitcast.17, bf16[512,128]{1,0:T(8,128)(2,1)} %bitcast.15, bf16[128,128]{1,0:T(8,128)(2,1)} %slice.15.gatew_ref, ...), custom_call_target="tpu_custom_call" | custom-call | flops 6499999744 | bytes 16000000 | tf_op jit(solution)/shard_map/pallas_call | solution.py:383
  211.1 4.9 %copy.18 = bf16[160,80,128]{2,1,0:T(8,128)(2,1)} copy(bf16[160,80,128]{2,0,1:T(8,128)(2,1)} %bitcast.12) | data formatting | bytes 6553600 | tf_op jit(solution)/shard_map/transpose | solution.py:421
  (4 shorter events, 0.0 us)

commit v2 on v1

v2 whole, which is shorter than its diff:
```python
import jax
import jax.numpy as jnp
from jax import lax
from jax.experimental import pallas as pl
from jax.experimental.pallas import tpu as pltpu
from jax.sharding import PartitionSpec as P

MESH = pl.DeviceIdType.MESH
F32 = jnp.float32
BF16 = jnp.bfloat16
epsilon = 1e-05

I = 160
K = 80
C = 128
G = 16
A = 8
N = 1280
REST = 24
FIRST = 48
R_MAIN, R_REST, L_REST, L_MAIN, T_REST, T_FIRST, T_LAST = range(7)


def kernel(
    x_ref,
    mask_ref,
    gain_ref,
    bias_ref,
    weights_ref,
    ogain_ref,
    obias_ref,
    ow_ref,
    o_ref,
    wide,
    normed,
    gates,
    swap,
    proj,
    mask_main,
    mask_rest,
    scaling,
    out_l,
    out_r,
    out_t,
    out_l_rest,
    out_r_rest,
    out_t_rest,
    in_l,
    in_r,
    in_t,
    in_l_rest,
    in_r_rest,
    in_t_rest,
    rest_l,
    rest_r,
    right_t,
    send_sem,
    recv_sem,
):
    g = lax.axis_index("grp")
    y = lax.axis_index("pr")
    core = lax.axis_index("pc")
    x, z = g // 4, g % 4
    a = y * 2 + core
    quarter = a % 4
    mine = g * A + a

    def partner(step):
        v = (step * 47) % 128
        px = (x + (0 + v % 4 + (v % 4) // 2 - 2 * ((v % 4) // 3))) % 4
        pcore = (core + (v // 4) % 2) % 2
        py = (y + (v // 8) % 4) % 4
        pz = (z + v // 32) % 4
        return px * 4 + pz, py, pcore

    def place(pg, py, pcore):
        return {"grp": pg, "pr": py, "pc": pcore}

    barrier = pltpu.get_barrier_semaphore()

    def greet(step, carry):
        pl.semaphore_signal(
            barrier, inc=1, device_id=place(*partner(step)), device_id_type=MESH
        )
        return carry

    lax.fori_loop(1, 128, greet, 0)

    def by_group(parts):
        group = lax.broadcasted_iota(jnp.int32, parts[0].shape, 1) // 32
        return jnp.where(
            group == 0,
            parts[0],
            jnp.where(group == 1, parts[1], jnp.where(group == 2, parts[2], parts[3])),
        )

    def token(s, r, low):
        n = (quarter - s + 4) % 4
        return n * 16 + r if low else 64 + n * 4 + r

    def by_16(value):
        return pl.multiple_of(value, 16)

    for part in range(4):
        columns = weights_ref[:, part * C : (part + 1) * C].astype(F32)
        proj[part * C : (part + 1) * C, :] = columns.T.astype(BF16)
    scaling[0] = jnp.broadcast_to(ogain_ref[...], (C, 128)).T
    scaling[1] = jnp.broadcast_to(obias_ref[...], (C, 128)).T
    mask = mask_ref[...].astype(F32).T
    mask_main[...] = mask[:, :128]
    mask_rest[...] = jnp.concatenate([mask[:, 128:]] * 4, axis=1)
    ones = jnp.full((256, 128), 1 / 128, BF16)

    def normalize(b):
        def rows(i, carry):
            block = x_ref[pl.ds(i * 8, 8), pl.ds(by_16(b * 16), 16), :].reshape(128, C)
            center = jnp.dot(block, ones[:128], preferred_element_type=F32)
            shifted = block.astype(F32) - center
            squares = shifted * shifted
            high = squares.astype(BF16)
            low = (squares - high.astype(F32)).astype(BF16)
            spread = jnp.dot(
                jnp.concatenate([high, low], axis=1), ones, preferred_element_type=F32
            )
            wide[pl.ds(i * 128, 128), :] = (
                shifted * lax.rsqrt(spread + epsilon) * gain_ref[...] + bias_ref[...]
            )
            return carry

        lax.fori_loop(0, I // 8, rows, 0, unroll=2)

        def turn(k, carry):
            normed[b * 16 + k] = wide[pl.ds(k, I, stride=16), :].astype(BF16)
            return carry

        lax.fori_loop(0, 16, turn, 0, unroll=2)

    def gated(tokens, weights, mask_rows):
        both = lax.dot_general(
            weights, tokens, (((1,), (1,)), ((), ())), preferred_element_type=F32
        )
        value, gate = both[:C], both[C:]
        return value * jax.nn.sigmoid(gate) * mask_rows

    def unswap(store, rows, at):
        def one(c, carry):
            store[c, pl.ds(at, rows), :] = swap[pl.ds(c, rows, stride=C), :].astype(BF16)
            return carry

        lax.fori_loop(0, C, one, 0, unroll=8)

    def project_main(b, first, store):
        weights = proj[first : first + 2 * C, :]

        def pair(p, carry):
            k = b * 16 + p * 2
            tokens = normed[pl.ds(k, 2), 0:128, :].reshape(256, C)
            rows = mask_main[pl.ds(k, 2), :]
            result = gated(tokens, weights, jnp.concatenate([rows[0:1], rows[1:2]], axis=1))
            swap[pl.ds(p * 256, C), :] = result[:, :128]
            swap[pl.ds(p * 256 + C, C), :] = result[:, 128:]
            return carry

        lax.fori_loop(0, 8, pair, 0)
        unswap(store, 16, by_16(b * 16))

    def rest_tokens(r, low):
        return jnp.concatenate([normed[token(s, r, low), 128:, :] for s in range(4)], axis=0)

    def rest_mask(r, low):
        return by_group([mask_rest[pl.ds(token(s, r, low), 1), :] for s in range(4)])

    def project_rest(first, store):
        weights = proj[first : first + 2 * C, :]
        for low, pairs, rows, at in ((True, 8, 16, 0), (False, 2, 8, 16)):

            def rest(p, carry):
                r = p * 2
                tokens = jnp.concatenate([rest_tokens(r, low), rest_tokens(r + 1, low)], axis=0)
                result = gated(
                    tokens,
                    weights,
                    jnp.concatenate([rest_mask(r, low), rest_mask(r + 1, low)], axis=1),
                )
                swap[pl.ds(p * 256, C), :] = result[:, :128]
                swap[pl.ds(p * 256 + C, C), :] = result[:, 128:]
                return carry

            lax.fori_loop(0, pairs, rest, 0)
            unswap(store, rows, at)

    def send_round(source, target, which):
        def one(step, carry):
            pg, py, pcore = partner(step)
            pltpu.make_async_remote_copy(
                src_ref=source(pg, py * 2 + pcore),
                dst_ref=target,
                send_sem=send_sem.at[which],
                recv_sem=recv_sem.at[which],
                device_id=place(pg, py, pcore),
                device_id_type=MESH,
            ).start()
            return carry

        pltpu.make_async_copy(source(g, a), target, recv_sem.at[which]).start()
        lax.fori_loop(1, 128, one, 0)

    def wait_all(buffer, semaphore):
        pltpu.make_async_copy(buffer, buffer, semaphore).wait()

    def send_main(b, store, target, which):
        send_round(
            lambda pg, pa: store.at[pg * A + pa, pl.ds(by_16(b * 16), 16)],
            target.at[a, pl.ds(by_16(g * K + b * 16), 16)],
            which,
        )

    def right_block(b, carry):
        normalize(b)
        project_main(b, 2 * C, out_r)

        @pl.when(b == 0)
        def _():
            pl.semaphore_wait(barrier, 127)

        send_main(b, out_r, in_r, R_MAIN)
        return carry

    lax.fori_loop(0, 5, right_block, 0)
    project_rest(2 * C, out_r_rest)
    send_round(lambda pg, pa: out_r_rest.at[pg * A + pa], in_r_rest.at[a, g], R_REST)
    project_rest(0, out_l_rest)
    send_round(lambda pg, pa: out_l_rest.at[pg * A + pa], in_l_rest.at[a, g], L_REST)

    def left_block(b, carry):
        project_main(b, 0, out_l)
        send_main(b, out_l, in_l, L_MAIN)
        return carry

    lax.fori_loop(0, 5, left_block, 0)

    def open_gate(p, carry):
        tokens = normed[pl.ds(p * 2, 2)].reshape(2 * I, C)
        gates[pl.ds(p * 2, 2)] = jax.nn.sigmoid(
            jnp.dot(tokens, weights_ref[:, 4 * C :], preferred_element_type=F32)
        ).reshape(2, I, C)
        return carry

    lax.fori_loop(0, K // 2, open_gate, 0)

    def spread_rest(arrived, rest):
        def one(step, carry):
            h, sg = step // G, step % G
            parts = [arrived[4 * h + t, sg, 0:16, :].astype(F32) for t in range(4)]
            tails = [arrived[4 * h + t, sg, 16:24, :].astype(F32) for t in range(4)]
            at = sg * K
            ends = []
            for n in range(4):
                rows = by_group([parts[(s + n) % 4] for s in range(4)])
                tail = by_group([tails[(s + n) % 4] for s in range(4)])
                if n:
                    rows = pltpu.roll(rows, 32 * n, 1)
                    tail = pltpu.roll(tail, 32 * n, 1)
                rest[h, pl.ds(by_16(at + n * 16), 16), :] = rows.astype(BF16)
                ends.append(tail)
            upper = lax.broadcasted_iota(jnp.int32, (8, 128), 0) < 4
            joined = jnp.concatenate(
                [
                    jnp.where(upper, ends[0], pltpu.roll(ends[1], 4, 0)),
                    jnp.where(upper, ends[2], pltpu.roll(ends[3], 4, 0)),
                ],
                axis=0,
            )
            rest[h, pl.ds(by_16(at + 64), 16), :] = joined.astype(BF16)
            return carry

        lax.fori_loop(0, 2 * G, one, 0)

    wait_all(in_r, recv_sem.at[R_MAIN])

    def turn_main(b, carry):
        right_t[pl.ds(pl.multiple_of(b * I, 32), 128), :] = in_r[b].T
        return carry

    lax.fori_loop(0, A, turn_main, 0)

    wait_all(in_r_rest, recv_sem.at[R_REST])
    spread_rest(in_r_rest, rest_r)

    def turn_rest(h, carry):
        turned = rest_r[h].T
        for t in range(4):
            right_t[pl.ds(pl.multiple_of((4 * h + t) * I + 128, 32), 32), :] = turned[
                32 * t : 32 * t + 32
            ]
        return carry

    lax.fori_loop(0, 2, turn_rest, 0)

    wait_all(in_l_rest, recv_sem.at[L_REST])
    spread_rest(in_l_rest, rest_l)

    def rest_product(m, carry):
        rows = right_t[pl.ds(pl.multiple_of(m * 320, 32), 320), :]
        columns = jnp.concatenate([rest_l[0], rest_l[1]], axis=1)
        product = jnp.dot(rows, columns, preferred_element_type=F32)
        for h in range(2):
            for sg in range(4):
                block = product[sg * K : (sg + 1) * K, h * 128 : (h + 1) * 128]
                mains, tails = [], []
                for n in range(4):
                    main = block[n * 16 : (n + 1) * 16]
                    tail = block[64 + 8 * (n // 2) : 72 + 8 * (n // 2)]
                    if n % 2:
                        tail = pltpu.roll(tail, 4, 0)
                    if n:
                        main = pltpu.roll(main, 128 - 32 * n, 1)
                        tail = pltpu.roll(tail, 128 - 32 * n, 1)
                    mains.append(main)
                    tails.append(tail)
                for t in range(4):
                    out_t_rest[m * 4 + sg, 4 * h + t, 0:16, :] = by_group(
                        [mains[(t - s) % 4] for s in range(4)]
                    ).astype(BF16)
                    out_t_rest[m * 4 + sg, 4 * h + t, 16:24, :] = by_group(
                        [tails[(t - s) % 4] for s in range(4)]
                    ).astype(BF16)
        return carry

    lax.fori_loop(0, 4, rest_product, 0)
    send_round(lambda pg, pa: out_t_rest.at[pg, pa], in_t_rest.at[mine], T_REST)

    wait_all(in_l, recv_sem.at[L_MAIN])

    def main_product(step, carry):
        i, j = step % 4, step // 4
        dx = (1 + 2 * i + i // 2) % 4
        dy = (3 * dx + j) % 4
        tx, ty = (x + dx) % 4, (y + dy) % 4
        rows = right_t[pl.ds(pl.multiple_of(tx * 320, 32), 320), :]
        columns = jnp.concatenate([in_l[2 * ty], in_l[2 * ty + 1]], axis=1)
        product = jnp.dot(rows, columns, preferred_element_type=F32).astype(BF16)
        for h in range(2):
            out_t[pl.ds(tx * 4, 4), 2 * ty + h] = product[
                :, h * 128 : (h + 1) * 128
            ].reshape(4, K, 128)

        def send(q, carry):
            pg, pcore = tx * 4 + (z + q // 2) % 4, (core + q % 2) % 2
            source = out_t.at[pg, 2 * ty + pcore, pl.ds(0, FIRST)]
            target = in_t.at[mine, pl.ds(0, FIRST)]
            own = (dx == 0) & (dy == 0) & (q == 0)

            @pl.when(own)
            def _():
                pltpu.make_async_copy(source, target, recv_sem.at[T_FIRST]).start()

            @pl.when(jnp.logical_not(own))
            def _():
                pltpu.make_async_remote_copy(
                    src_ref=source,
                    dst_ref=target,
                    send_sem=send_sem.at[T_FIRST],
                    recv_sem=recv_sem.at[T_FIRST],
                    device_id=place(pg, ty, pcore),
                    device_id_type=MESH,
                ).start()

            return carry

        lax.fori_loop(0, 8, send, 0)
        return carry

    lax.fori_loop(0, 16, main_product, 0)
    last = pl.ds(FIRST, K - FIRST)
    send_round(lambda pg, pa: out_t.at[pg, pa, last], in_t.at[mine, last], T_LAST)

    def settle(r, rows):
        values = swap[pl.ds(r, C, stride=rows), :]
        center = jnp.mean(values, axis=0, keepdims=True)
        shifted = values - center
        spread = jnp.mean(shifted * shifted, axis=0, keepdims=True)
        settled = (shifted * lax.rsqrt(spread + epsilon) * scaling[0] + scaling[1]).astype(BF16)
        return lax.dot_general(
            settled, ow_ref[...], (((0,), (0,)), ((), ())), preferred_element_type=F32
        )

    def widen(arrived, at, rows):
        def one(c, carry):
            swap[pl.ds(pl.multiple_of(c * rows, 8), rows), :] = arrived[
                c, pl.ds(at, rows), :
            ].astype(F32)
            return carry

        lax.fori_loop(0, C, one, 0, unroll=8)

    def finish(b, carry):
        widen(in_t, by_16(b * 16), 16)

        def one(r, carry):
            j = b * 16 + r
            o_ref[j, 0:128, :] = (gates[j, 0:128, :] * settle(r, 16)).astype(BF16)
            return carry

        lax.fori_loop(0, 16, one, 0, unroll=4)
        return carry

    wait_all(in_t_rest, recv_sem.at[T_REST])
    for low, count, rows, at in ((True, 16, 16, 0), (False, 4, 8, 16)):
        widen(in_t_rest, at, rows)

        def one_rest(r, carry):
            mixed = settle(r, rows)
            for s in range(4):
                j = token(s, r, low)
                o_ref[j, 128:, :] = (
                    gates[j, 128:, :] * mixed[32 * s : 32 * s + 32]
                ).astype(BF16)
            return carry

        lax.fori_loop(0, count, one_rest, 0, unroll=4)

    wait_all(in_t.at[:, pl.ds(0, FIRST)], recv_sem.at[T_FIRST])
    lax.fori_loop(0, FIRST // 16, finish, 0)
    wait_all(in_t.at[:, last], recv_sem.at[T_LAST])
    lax.fori_loop(FIRST // 16, K // 16, finish, 0)

    for which, buffer in (
        (R_MAIN, out_r),
        (R_REST, out_r_rest),
        (L_REST, out_l_rest),
        (L_MAIN, out_l),
        (T_REST, in_t_rest),
        (T_FIRST, in_t.at[:, pl.ds(0, FIRST)]),
        (T_LAST, in_t.at[:, last]),
    ):
        wait_all(buffer.at[pl.ds(0, 127)], send_sem.at[which])


def per_device(
    pair_map,
    pair_mask,
    input_gain,
    input_bias,
    input_weights,
    output_gain,
    output_bias,
    output_weight,
):
    vmem = pl.BlockSpec(memory_space=pltpu.VMEM)
    result = pl.pallas_call(
        kernel,
        out_shape=jax.ShapeDtypeStruct((K, I, C), BF16),
        in_specs=[vmem] * 8,
        out_specs=vmem,
        scratch_shapes=[
            pltpu.VMEM((I * 16, C), F32),
            pltpu.VMEM((K, I, C), BF16),
            pltpu.VMEM((K, I, C), F32),
            pltpu.VMEM((16 * C, 128), F32),
            pltpu.VMEM((4 * C, C), BF16),
            pltpu.VMEM((K, 128), F32),
            pltpu.VMEM((K, 128), F32),
            pltpu.VMEM((2, C, 128), F32),
            pltpu.VMEM((C, K, 128), BF16),
            pltpu.VMEM((C, K, 128), BF16),
            pltpu.VMEM((G, A, K, 128), BF16),
            pltpu.VMEM((C, REST, 128), BF16),
            pltpu.VMEM((C, REST, 128), BF16),
            pltpu.VMEM((G, A, REST, 128), BF16),
            pltpu.VMEM((A, N, 128), BF16),
            pltpu.VMEM((A, N, 128), BF16),
            pltpu.VMEM((C, K, 128), BF16),
            pltpu.VMEM((A, G, REST, 128), BF16),
            pltpu.VMEM((A, G, REST, 128), BF16),
            pltpu.VMEM((C, REST, 128), BF16),
            pltpu.VMEM((2, N, 128), BF16),
            pltpu.VMEM((2, N, 128), BF16),
            pltpu.VMEM((N, N), BF16),
            pltpu.SemaphoreType.DMA((7,)),
            pltpu.SemaphoreType.DMA((7,)),
        ],
        compiler_params=pltpu.CompilerParams(
            collective_id=0, has_side_effects=True, vmem_limit_bytes=58 * 2**20
        ),
        cost_estimate=pl.CostEstimate(
            flops=6_500_000_000, bytes_accessed=16_000_000, transcendentals=5_000_000
        ),
    )(
        pair_map,
        pair_mask,
        input_gain[None],
        input_bias[None],
        input_weights,
        output_gain[None],
        output_bias[None],
        output_weight,
    )
    return jnp.transpose(result, (1, 0, 2))


def solution(mesh):
    return jax.shard_map(
        per_device,
        mesh=mesh,
        in_specs=(
            P(("pr", "pc"), "grp", None),
            P(("pr", "pc"), "grp"),
            P(),
            P(),
            P(),
            P(),
            P(),
            P(),
        ),
        out_specs=P(("pr", "pc"), "grp", None),
        check_vma=False,
    )
```

time: 216 us -> 207 us (0.958)
  local copies, waits for them, and re-layouts: 16.3 us -> 4.9 us
  Pallas kernels: 199 us -> 202 us
    unnamed x3 -> x0, local copies, waits for them, and re-layouts: 6.19 us -> none
    pallas_call x1, Pallas kernels: 199 us -> 202 us  [per_device(): pl.pallas_call(kernel, out_shape=jax.ShapeDtypeStruct((K, I, C), BF16), i...]
    broadcast_in_dim x2 -> x0, local copies, waits for them, and re-layouts: 2.74 us -> none  [the longest x1 1.37 us: per_device(): offsets = jnp.broadcast_to(output_bias[:, None], (C, 128))]
    slice x4 -> x0, local copies, waits for them, and re-layouts: 2.34 us -> none  [the longest x1 1.36 us: per_device(): gate_weights = input_weights[:, 4 * C:]]
where the time goes in v2:
time: 207 us
  Pallas kernels  202 us (98%)
  local copies, waits for them, and re-layouts  4.9 us (2%)
    pallas_call x1, Pallas kernels, per_device(): pl.pallas_call(kernel, out_shape=jax.ShapeDtypeStruct((K, I, C), BF16), i...  202 us
    transpose x1, local copies, waits for them, and re-layouts, per_device(): return jnp.transpose(result, (1, 0, 2))  4.9 us

profile of v2, /device:TPU:1, one launch (start us, length us, event | category | flops | bytes accessed | tf_op | source)
XLA Modules:
  0.0 207.4 jit_solution(11184303912630686470)
XLA Ops:
  0.0 202.4 %shard_map.82 = bf16[80,160,128]{2,1,0:T(8,128)(2,1)} custom-call(bf16[160,80,128]{2,1,0:T(8,128)(2,1)} %x_ref.1, s32[160,80]{1,0:T(8,128)} %mask_ref.1, f32[1,128]{1,0:T(1,128)} %bitcast.6, f32[1,128]{1,0:T(1,128)} %bitcast.7, bf16[128,640]{1,0:T(8,128)(2,1)} %weights_ref.1, f32[1,128]{1,0:T(1,128)} %bitcast.8, f32[1,128]{1,0:T(1,128)} %bitcast.9, ...), custom_call_target="tpu_custom_call" | custom-call | flops 6499999744 | bytes 16000000 | tf_op jit(solution)/shard_map/pallas_call | solution.py:451
  202.5 4.9 %copy.9 = bf16[160,80,128]{2,1,0:T(8,128)(2,1)} copy(bf16[160,80,128]{2,0,1:T(8,128)(2,1)} %bitcast.5) | data formatting | bytes 6553600 | tf_op jit(solution)/shard_map/transpose | solution.py:499

commit v3 on v2

--- a/solution.py
+++ b/solution.py
@@ -17,8 +17,9 @@
 A = 8
 N = 1280
 REST = 24
+BOTH = 40
 FIRST = 48
-R_MAIN, R_REST, L_REST, L_MAIN, T_REST, T_FIRST, T_LAST = range(7)
+R_MAIN, BOTH_REST, L_MAIN, T_REST, T_FIRST, T_LAST = range(6)
 
 
 def kernel(
@@ -42,14 +43,12 @@
     out_l,
     out_r,
     out_t,
-    out_l_rest,
-    out_r_rest,
+    out_rest,
     out_t_rest,
     in_l,
     in_r,
     in_t,
-    in_l_rest,
-    in_r_rest,
+    in_rest,
     in_t_rest,
     rest_l,
     rest_r,
@@ -60,17 +59,18 @@
     g = lax.axis_index("grp")
     y = lax.axis_index("pr")
     core = lax.axis_index("pc")
-    x, z = g // 4, g % 4
+    x, z = g >> 2, g & 3
     a = y * 2 + core
-    quarter = a % 4
+    quarter = a & 3
     mine = g * A + a
 
     def partner(step):
-        v = (step * 47) % 128
-        px = (x + (0 + v % 4 + (v % 4) // 2 - 2 * ((v % 4) // 3))) % 4
-        pcore = (core + (v // 4) % 2) % 2
-        py = (y + (v // 8) % 4) % 4
-        pz = (z + v // 32) % 4
+        v = (step * 47) & 127
+        w = v & 3
+        px = (x + (w ^ (w >> 1))) & 3
+        pcore = core ^ ((v >> 2) & 1)
+        py = (y + (v >> 3)) & 3
+        pz = (z + (v >> 5)) & 3
         return px * 4 + pz, py, pcore
 
     def place(pg, py, pcore):
@@ -78,13 +78,21 @@
 
     barrier = pltpu.get_barrier_semaphore()
 
-    def greet(step, carry):
+    def each_partner(visit):
+        def several(n, carry):
+            for u in range(7):
+                visit(*partner(n * 7 + u + 1))
+            return carry
+
+        lax.fori_loop(0, 18, several, 0)
+        visit(*partner(127))
+
+    def greet(pg, py, pcore):
         pl.semaphore_signal(
-            barrier, inc=1, device_id=place(*partner(step)), device_id_type=MESH
-        )
-        return carry
-
-    lax.fori_loop(1, 128, greet, 0)
+            barrier, inc=1, device_id=place(pg, py, pcore), device_id_type=MESH
+        )
+
+    each_partner(greet)
 
     def by_group(parts):
         group = lax.broadcasted_iota(jnp.int32, parts[0].shape, 1) // 32
@@ -95,7 +103,7 @@
         )
 
     def token(s, r, low):
-        n = (quarter - s + 4) % 4
+        n = (quarter - s + 4) & 3
         return n * 16 + r if low else 64 + n * 4 + r
 
     def by_16(value):
@@ -113,7 +121,7 @@
 
     def normalize(b):
         def rows(i, carry):
-            block = x_ref[pl.ds(i * 8, 8), pl.ds(by_16(b * 16), 16), :].reshape(128, C)
+            block = x_ref[pl.ds(i * 32, 32), pl.ds(by_16(b * 16), 16), :].reshape(512, C)
             center = jnp.dot(block, ones[:128], preferred_element_type=F32)
             shifted = block.astype(F32) - center
             squares = shifted * shifted
@@ -122,12 +130,12 @@
             spread = jnp.dot(
                 jnp.concatenate([high, low], axis=1), ones, preferred_element_type=F32
             )
-            wide[pl.ds(i * 128, 128), :] = (
+            wide[pl.ds(i * 512, 512), :] = (
                 shifted * lax.rsqrt(spread + epsilon) * gain_ref[...] + bias_ref[...]
             )
             return carry
 
-        lax.fori_loop(0, I // 8, rows, 0, unroll=2)
+        lax.fori_loop(0, I // 32, rows, 0)
 
         def turn(k, carry):
             normed[b * 16 + k] = wide[pl.ds(k, I, stride=16), :].astype(BF16)
@@ -142,27 +150,14 @@
         value, gate = both[:C], both[C:]
         return value * jax.nn.sigmoid(gate) * mask_rows
 
-    def unswap(store, rows, at):
-        def one(c, carry):
-            store[c, pl.ds(at, rows), :] = swap[pl.ds(c, rows, stride=C), :].astype(BF16)
-            return carry
-
-        lax.fori_loop(0, C, one, 0, unroll=8)
-
-    def project_main(b, first, store):
-        weights = proj[first : first + 2 * C, :]
-
-        def pair(p, carry):
-            k = b * 16 + p * 2
-            tokens = normed[pl.ds(k, 2), 0:128, :].reshape(256, C)
-            rows = mask_main[pl.ds(k, 2), :]
-            result = gated(tokens, weights, jnp.concatenate([rows[0:1], rows[1:2]], axis=1))
-            swap[pl.ds(p * 256, C), :] = result[:, :128]
-            swap[pl.ds(p * 256 + C, C), :] = result[:, 128:]
-            return carry
-
-        lax.fori_loop(0, 8, pair, 0)
-        unswap(store, 16, by_16(b * 16))
+    def project_main(k, at, first):
+        tokens = normed[pl.ds(k, 2), 0:128, :].reshape(256, C)
+        rows = mask_main[pl.ds(k, 2), :]
+        result = gated(
+            tokens, proj[first : first + 2 * C, :], jnp.concatenate([rows[0:1], rows[1:2]], axis=1)
+        )
+        swap[pl.ds(at * C, C), :] = result[:, :128]
+        swap[pl.ds(at * C + C, C), :] = result[:, 128:]
 
     def rest_tokens(r, low):
         return jnp.concatenate([normed[token(s, r, low), 128:, :] for s in range(4)], axis=0)
@@ -170,74 +165,98 @@
     def rest_mask(r, low):
         return by_group([mask_rest[pl.ds(token(s, r, low), 1), :] for s in range(4)])
 
-    def project_rest(first, store):
-        weights = proj[first : first + 2 * C, :]
-        for low, pairs, rows, at in ((True, 8, 16, 0), (False, 2, 8, 16)):
-
-            def rest(p, carry):
-                r = p * 2
-                tokens = jnp.concatenate([rest_tokens(r, low), rest_tokens(r + 1, low)], axis=0)
-                result = gated(
-                    tokens,
-                    weights,
-                    jnp.concatenate([rest_mask(r, low), rest_mask(r + 1, low)], axis=1),
-                )
-                swap[pl.ds(p * 256, C), :] = result[:, :128]
-                swap[pl.ds(p * 256 + C, C), :] = result[:, 128:]
-                return carry
-
-            lax.fori_loop(0, pairs, rest, 0)
-            unswap(store, rows, at)
-
-    def send_round(source, target, which):
-        def one(step, carry):
-            pg, py, pcore = partner(step)
+    def project_rest(r, at, low, first):
+        tokens = jnp.concatenate([rest_tokens(r, low), rest_tokens(r + 1, low)], axis=0)
+        result = gated(
+            tokens,
+            proj[first : first + 2 * C, :],
+            jnp.concatenate([rest_mask(r, low), rest_mask(r + 1, low)], axis=1),
+        )
+        swap[pl.ds(at * C, C), :] = result[:, :128]
+        swap[pl.ds(at * C + C, C), :] = result[:, 128:]
+
+    def ready(c):
+        return
+
+    def send_round(prepare, source, target, which):
+        def one(pg, py, pcore):
+            pa = py * 2 + pcore
+            prepare(pg * A + pa)
             pltpu.make_async_remote_copy(
-                src_ref=source(pg, py * 2 + pcore),
+                src_ref=source(pg, pa),
                 dst_ref=target,
                 send_sem=send_sem.at[which],
                 recv_sem=recv_sem.at[which],
                 device_id=place(pg, py, pcore),
                 device_id_type=MESH,
             ).start()
-            return carry
-
+
+        prepare(mine)
         pltpu.make_async_copy(source(g, a), target, recv_sem.at[which]).start()
-        lax.fori_loop(1, 128, one, 0)
+        each_partner(one)
 
     def wait_all(buffer, semaphore):
         pltpu.make_async_copy(buffer, buffer, semaphore).wait()
 
-    def send_main(b, store, target, which):
+    def send_main(start, rows, store, target, which):
+        from_row = pl.ds(by_16(start), rows)
+
+        def prepare(c):
+            store[c, from_row, :] = swap[pl.ds(c, rows, stride=C), :].astype(BF16)
+
         send_round(
-            lambda pg, pa: store.at[pg * A + pa, pl.ds(by_16(b * 16), 16)],
-            target.at[a, pl.ds(by_16(g * K + b * 16), 16)],
+            prepare,
+            lambda pg, pa: store.at[pg * A + pa, from_row],
+            target.at[a, pl.ds(by_16(g * K + start), rows)],
             which,
         )
 
+    def project_rows(start, count, first):
+        def pair(p, carry):
+            project_main(start + p * 2, p * 2, first)
+            return carry
+
+        lax.fori_loop(0, count // 2, pair, 0)
+
+    normalize(0)
+    project_rows(0, 16, 2 * C)
+    pl.semaphore_wait(barrier, 127)
+    send_main(0, 16, out_r, in_r, R_MAIN)
+
     def right_block(b, carry):
-        normalize(b)
-        project_main(b, 2 * C, out_r)
-
-        @pl.when(b == 0)
-        def _():
-            pl.semaphore_wait(barrier, 127)
-
-        send_main(b, out_r, in_r, R_MAIN)
-        return carry
-
-    lax.fori_loop(0, 5, right_block, 0)
-    project_rest(2 * C, out_r_rest)
-    send_round(lambda pg, pa: out_r_rest.at[pg * A + pa], in_r_rest.at[a, g], R_REST)
-    project_rest(0, out_l_rest)
-    send_round(lambda pg, pa: out_l_rest.at[pg * A + pa], in_l_rest.at[a, g], L_REST)
-
-    def left_block(b, carry):
-        project_main(b, 0, out_l)
-        send_main(b, out_l, in_l, L_MAIN)
-        return carry
-
-    lax.fori_loop(0, 5, left_block, 0)
+        normalize(2 * b + 1)
+        normalize(2 * b + 2)
+        start = 32 * b + 16
+        project_rows(start, 32, 2 * C)
+        send_main(start, 32, out_r, in_r, R_MAIN)
+        return carry
+
+    lax.fori_loop(0, 2, right_block, 0)
+
+    def low_rest(p, carry):
+        project_rest(p * 2, p * 2, True, 2 * C)
+        project_rest(p * 2, 16 + p * 2, True, 0)
+        return carry
+
+    lax.fori_loop(0, 8, low_rest, 0)
+
+    def high_rest(p, carry):
+        project_rest(p * 2, 32 + p * 2, False, 2 * C)
+        project_rest(p * 2, 36 + p * 2, False, 0)
+        return carry
+
+    lax.fori_loop(0, 2, high_rest, 0)
+
+    def prepare_rest(c):
+        out_rest[c] = swap[pl.ds(c, BOTH, stride=C), :].astype(BF16)
+
+    send_round(
+        prepare_rest, lambda pg, pa: out_rest.at[pg * A + pa], in_rest.at[a, g], BOTH_REST
+    )
+
+    for start, count in ((0, 32), (32, 48)):
+        project_rows(start, count, 0)
+        send_main(start, count, out_l, in_l, L_MAIN)
 
     def open_gate(p, carry):
         tokens = normed[pl.ds(p * 2, 2)].reshape(2 * I, C)
@@ -248,11 +267,15 @@
 
     lax.fori_loop(0, K // 2, open_gate, 0)
 
-    def spread_rest(arrived, rest):
+    def spread_rest(side, rest):
         def one(step, carry):
-            h, sg = step // G, step % G
-            parts = [arrived[4 * h + t, sg, 0:16, :].astype(F32) for t in range(4)]
-            tails = [arrived[4 * h + t, sg, 16:24, :].astype(F32) for t in range(4)]
+            h, sg = step >> 4, step & 15
+            parts = [
+                in_rest[4 * h + t, sg, 16 * side : 16 * side + 16, :].astype(F32) for t in range(4)
+            ]
+            tails = [in_rest[4 * h + t, sg, 32:40, :].astype(F32) for t in range(4)]
+            if side:
+                tails = [pltpu.roll(tail, 4, 0) for tail in tails]
             at = sg * K
             ends = []
             for n in range(4):
@@ -284,8 +307,8 @@
 
     lax.fori_loop(0, A, turn_main, 0)
 
-    wait_all(in_r_rest, recv_sem.at[R_REST])
-    spread_rest(in_r_rest, rest_r)
+    wait_all(in_rest, recv_sem.at[BOTH_REST])
+    spread_rest(0, rest_r)
 
     def turn_rest(h, carry):
         turned = rest_r[h].T
@@ -297,8 +320,7 @@
 
     lax.fori_loop(0, 2, turn_rest, 0)
 
-    wait_all(in_l_rest, recv_sem.at[L_REST])
-    spread_rest(in_l_rest, rest_l)
+    spread_rest(1, rest_l)
 
     def rest_product(m, carry):
         rows = right_t[pl.ds(pl.multiple_of(m * 320, 32), 320), :]
@@ -328,15 +350,15 @@
         return carry
 
     lax.fori_loop(0, 4, rest_product, 0)
-    send_round(lambda pg, pa: out_t_rest.at[pg, pa], in_t_rest.at[mine], T_REST)
+    send_round(ready, lambda pg, pa: out_t_rest.at[pg, pa], in_t_rest.at[mine], T_REST)
 
     wait_all(in_l, recv_sem.at[L_MAIN])
 
     def main_product(step, carry):
-        i, j = step % 4, step // 4
-        dx = (1 + 2 * i + i // 2) % 4
-        dy = (3 * dx + j) % 4
-        tx, ty = (x + dx) % 4, (y + dy) % 4
+        i, j = step & 3, step >> 2
+        dx = (1 + 2 * i + (i >> 1)) & 3
+        dy = (3 * dx + j) & 3
+        tx, ty = (x + dx) & 3, (y + dy) & 3
         rows = right_t[pl.ds(pl.multiple_of(tx * 320, 32), 320), :]
         columns = jnp.concatenate([in_l[2 * ty], in_l[2 * ty + 1]], axis=1)
         product = jnp.dot(rows, columns, preferred_element_type=F32).astype(BF16)
@@ -346,7 +368,7 @@
             ].reshape(4, K, 128)
 
         def send(q, carry):
-            pg, pcore = tx * 4 + (z + q // 2) % 4, (core + q % 2) % 2
+            pg, pcore = tx * 4 + ((z + (q >> 1)) & 3), core ^ (q & 1)
             source = out_t.at[pg, 2 * ty + pcore, pl.ds(0, FIRST)]
             target = in_t.at[mine, pl.ds(0, FIRST)]
             own = (dx == 0) & (dy == 0) & (q == 0)
@@ -373,7 +395,7 @@
 
     lax.fori_loop(0, 16, main_product, 0)
     last = pl.ds(FIRST, K - FIRST)
-    send_round(lambda pg, pa: out_t.at[pg, pa, last], in_t.at[mine, last], T_LAST)
+    send_round(ready, lambda pg, pa: out_t.at[pg, pa, last], in_t.at[mine, last], T_LAST)
 
     def settle(r, rows):
         values = swap[pl.ds(r, C, stride=rows), :]
@@ -427,8 +449,7 @@
 
     for which, buffer in (
         (R_MAIN, out_r),
-        (R_REST, out_r_rest),
-        (L_REST, out_l_rest),
+        (BOTH_REST, out_rest),
         (L_MAIN, out_l),
         (T_REST, in_t_rest),
         (T_FIRST, in_t.at[:, pl.ds(0, FIRST)]),
@@ -457,7 +478,7 @@
             pltpu.VMEM((I * 16, C), F32),
             pltpu.VMEM((K, I, C), BF16),
             pltpu.VMEM((K, I, C), F32),
-            pltpu.VMEM((16 * C, 128), F32),
+            pltpu.VMEM((48 * C, 128), F32),
             pltpu.VMEM((4 * C, C), BF16),
             pltpu.VMEM((K, 128), F32),
             pltpu.VMEM((K, 128), F32),
@@ -465,20 +486,18 @@
             pltpu.VMEM((C, K, 128), BF16),
             pltpu.VMEM((C, K, 128), BF16),
             pltpu.VMEM((G, A, K, 128), BF16),
-            pltpu.VMEM((C, REST, 128), BF16),
-            pltpu.VMEM((C, REST, 128), BF16),
+            pltpu.VMEM((C, BOTH, 128), BF16),
             pltpu.VMEM((G, A, REST, 128), BF16),
             pltpu.VMEM((A, N, 128), BF16),
             pltpu.VMEM((A, N, 128), BF16),
             pltpu.VMEM((C, K, 128), BF16),
-            pltpu.VMEM((A, G, REST, 128), BF16),
-            pltpu.VMEM((A, G, REST, 128), BF16),
+            pltpu.VMEM((A, G, BOTH, 128), BF16),
             pltpu.VMEM((C, REST, 128), BF16),
             pltpu.VMEM((2, N, 128), BF16),
             pltpu.VMEM((2, N, 128), BF16),
             pltpu.VMEM((N, N), BF16),
-            pltpu.SemaphoreType.DMA((7,)),
-            pltpu.SemaphoreType.DMA((7,)),
+            pltpu.SemaphoreType.DMA((6,)),
+            pltpu.SemaphoreType.DMA((6,)),
         ],
         compiler_params=pltpu.CompilerParams(
             collective_id=0, has_side_effects=True, vmem_limit_bytes=58 * 2**20

time: 207 us -> 143 us (0.69)
  the two profiles are of different devices: /device:TPU:1 before, /device:TPU:5 now
where the time goes in v3:
time: 143 us
  Pallas kernels  138 us (97%)
  local copies, waits for them, and re-layouts  4.9 us (3%)
    pallas_call x1, Pallas kernels, per_device(): pl.pallas_call(kernel, out_shape=jax.ShapeDtypeStruct((K, I, C), BF16), i...  138 us
    transpose x1, local copies, waits for them, and re-layouts, per_device(): return jnp.transpose(result, (1, 0, 2))  4.9 us

profile of v3, /device:TPU:5, one launch (start us, length us, event | category | flops | bytes accessed | tf_op | source)
XLA Modules:
  0.0 143.0 jit_solution(10199257423711550601)
XLA Ops:
  0.0 138.1 %shard_map.82 = bf16[80,160,128]{2,1,0:T(8,128)(2,1)} custom-call(bf16[160,80,128]{2,1,0:T(8,128)(2,1)} %x_ref.1, s32[160,80]{1,0:T(8,128)} %mask_ref.1, f32[1,128]{1,0:T(1,128)} %bitcast.6, f32[1,128]{1,0:T(1,128)} %bitcast.7, bf16[128,640]{1,0:T(8,128)(2,1)} %weights_ref.1, f32[1,128]{1,0:T(1,128)} %bitcast.8, f32[1,128]{1,0:T(1,128)} %bitcast.9, ...), custom_call_target="tpu_custom_call" | custom-call | flops 6499999744 | bytes 16000000 | tf_op jit(solution)/shard_map/pallas_call | solution.py:472
  138.1 4.9 %copy.9 = bf16[160,80,128]{2,1,0:T(8,128)(2,1)} copy(bf16[160,80,128]{2,0,1:T(8,128)(2,1)} %bitcast.5) | data formatting | bytes 6553600 | tf_op jit(solution)/shard_map/transpose | solution.py:518

commit v4 on v3

--- a/solution.py
+++ b/solution.py
@@ -18,12 +18,12 @@
 N = 1280
 REST = 24
 BOTH = 40
-FIRST = 48
+FIRST = 64
 R_MAIN, BOTH_REST, L_MAIN, T_REST, T_FIRST, T_LAST = range(6)
 
 
 def kernel(
-    x_ref,
+    x_hbm,
     mask_ref,
     gain_ref,
     bias_ref,
@@ -31,12 +31,15 @@
     ogain_ref,
     obias_ref,
     ow_ref,
+    o_hbm,
+    x_ref,
     o_ref,
     wide,
     normed,
     gates,
     swap,
     proj,
+    gate_weights,
     mask_main,
     mask_rest,
     scaling,
@@ -53,6 +56,9 @@
     rest_l,
     rest_r,
     right_t,
+    fetch_sem,
+    store_sem,
+    entry_sem,
     send_sem,
     recv_sem,
 ):
@@ -87,12 +93,30 @@
         lax.fori_loop(0, 18, several, 0)
         visit(*partner(127))
 
-    def greet(pg, py, pcore):
+    def greet_row(semaphore):
+        for step in range(1, A):
+            pl.semaphore_signal(
+                semaphore,
+                inc=1,
+                device_id=place(g, (y + (step >> 1)) & 3, core ^ (step & 1)),
+                device_id_type=MESH,
+            )
+
+    def greet_column(step, carry):
         pl.semaphore_signal(
-            barrier, inc=1, device_id=place(pg, py, pcore), device_id_type=MESH
-        )
-
-    each_partner(greet)
+            barrier, inc=1, device_id=place((g + step) & 15, y, core), device_id_type=MESH
+        )
+        return carry
+
+    lax.fori_loop(1, G, greet_column, 0, unroll=5)
+    greet_row(barrier)
+
+    def fetch(b):
+        block = pl.ds(b * 16, 16)
+        return pltpu.make_async_copy(x_hbm.at[:, block], x_ref.at[:, block], fetch_sem.at[b])
+
+    for b in range(5):
+        fetch(b).start()
 
     def by_group(parts):
         group = lax.broadcasted_iota(jnp.int32, parts[0].shape, 1) // 32
@@ -111,7 +135,8 @@
 
     for part in range(4):
         columns = weights_ref[:, part * C : (part + 1) * C].astype(F32)
-        proj[part * C : (part + 1) * C, :] = columns.T.astype(BF16)
+        proj[part * C : (part + 1) * C, :] = (0.5 * columns.T).astype(BF16)
+    gate_weights[...] = (0.5 * weights_ref[:, 4 * C :].astype(F32)).astype(BF16)
     scaling[0] = jnp.broadcast_to(ogain_ref[...], (C, 128)).T
     scaling[1] = jnp.broadcast_to(obias_ref[...], (C, 128)).T
     mask = mask_ref[...].astype(F32).T
@@ -147,8 +172,8 @@
         both = lax.dot_general(
             weights, tokens, (((1,), (1,)), ((), ())), preferred_element_type=F32
         )
-        value, gate = both[:C], both[C:]
-        return value * jax.nn.sigmoid(gate) * mask_rows
+        half_value, half_gate = both[:C], both[C:]
+        return (half_value + half_value * jnp.tanh(half_gate)) * mask_rows
 
     def project_main(k, at, first):
         tokens = normed[pl.ds(k, 2), 0:128, :].reshape(256, C)
@@ -218,20 +243,28 @@
 
         lax.fori_loop(0, count // 2, pair, 0)
 
+    def left_rows(start, count):
+        project_rows(start, count, 0)
+        send_main(start, count, out_l, in_l, L_MAIN)
+
+    def right_rows(start, count):
+        project_rows(start, count, 2 * C)
+        send_main(start, count, out_r, in_r, R_MAIN)
+
+    fetch(0).wait()
     normalize(0)
+    pl.semaphore_wait(barrier, G + A - 2)
+    greet_row(entry_sem)
     project_rows(0, 16, 2 * C)
-    pl.semaphore_wait(barrier, 127)
+    pl.semaphore_wait(entry_sem, A - 1)
     send_main(0, 16, out_r, in_r, R_MAIN)
-
-    def right_block(b, carry):
+    left_rows(0, 16)
+    for b in range(2):
+        fetch(2 * b + 1).wait()
         normalize(2 * b + 1)
+        fetch(2 * b + 2).wait()
         normalize(2 * b + 2)
-        start = 32 * b + 16
-        project_rows(start, 32, 2 * C)
-        send_main(start, 32, out_r, in_r, R_MAIN)
-        return carry
-
-    lax.fori_loop(0, 2, right_block, 0)
+        right_rows(32 * b + 16, 32)
 
     def low_rest(p, carry):
         project_rest(p * 2, p * 2, True, 2 * C)
@@ -254,15 +287,13 @@
         prepare_rest, lambda pg, pa: out_rest.at[pg * A + pa], in_rest.at[a, g], BOTH_REST
     )
 
-    for start, count in ((0, 32), (32, 48)):
-        project_rows(start, count, 0)
-        send_main(start, count, out_l, in_l, L_MAIN)
+    left_rows(16, 32)
+    left_rows(48, 32)
 
     def open_gate(p, carry):
         tokens = normed[pl.ds(p * 2, 2)].reshape(2 * I, C)
-        gates[pl.ds(p * 2, 2)] = jax.nn.sigmoid(
-            jnp.dot(tokens, weights_ref[:, 4 * C :], preferred_element_type=F32)
-        ).reshape(2, I, C)
+        half = jnp.dot(tokens, gate_weights[...], preferred_element_type=F32)
+        gates[pl.ds(p * 2, 2)] = (0.5 + 0.5 * jnp.tanh(half)).reshape(2, I, C)
         return carry
 
     lax.fori_loop(0, K // 2, open_gate, 0)
@@ -444,8 +475,14 @@
 
     wait_all(in_t.at[:, pl.ds(0, FIRST)], recv_sem.at[T_FIRST])
     lax.fori_loop(0, FIRST // 16, finish, 0)
+
+    def put(number, block):
+        return pltpu.make_async_copy(o_ref.at[block], o_hbm.at[block], store_sem.at[number])
+
+    put(0, pl.ds(0, FIRST)).start()
     wait_all(in_t.at[:, last], recv_sem.at[T_LAST])
     lax.fori_loop(FIRST // 16, K // 16, finish, 0)
+    put(1, last).start()
 
     for which, buffer in (
         (R_MAIN, out_r),
@@ -456,6 +493,8 @@
         (T_LAST, in_t.at[:, last]),
     ):
         wait_all(buffer.at[pl.ds(0, 127)], send_sem.at[which])
+    put(0, pl.ds(0, FIRST)).wait()
+    put(1, last).wait()
 
 
 def per_device(
@@ -472,14 +511,17 @@
     result = pl.pallas_call(
         kernel,
         out_shape=jax.ShapeDtypeStruct((K, I, C), BF16),
-        in_specs=[vmem] * 8,
-        out_specs=vmem,
+        in_specs=[pl.BlockSpec(memory_space=pl.ANY)] + [vmem] * 7,
+        out_specs=pl.BlockSpec(memory_space=pl.ANY),
         scratch_shapes=[
+            pltpu.VMEM((I, K, C), BF16),
+            pltpu.VMEM((K, I, C), BF16),
             pltpu.VMEM((I * 16, C), F32),
             pltpu.VMEM((K, I, C), BF16),
             pltpu.VMEM((K, I, C), F32),
             pltpu.VMEM((48 * C, 128), F32),
             pltpu.VMEM((4 * C, C), BF16),
+            pltpu.VMEM((C, C), BF16),
             pltpu.VMEM((K, 128), F32),
             pltpu.VMEM((K, 128), F32),
             pltpu.VMEM((2, C, 128), F32),
@@ -496,6 +538,9 @@
             pltpu.VMEM((2, N, 128), BF16),
             pltpu.VMEM((2, N, 128), BF16),
             pltpu.VMEM((N, N), BF16),
+            pltpu.SemaphoreType.DMA((5,)),
+            pltpu.SemaphoreType.DMA((2,)),
+            pltpu.SemaphoreType.REGULAR,
             pltpu.SemaphoreType.DMA((6,)),
             pltpu.SemaphoreType.DMA((6,)),
         ],

time: 143 us -> 136 us (0.951)
  the two profiles are of different devices: /device:TPU:5 before, /device:TPU:1 now
where the time goes in v4:
time: 136 us
  Pallas kernels  131 us (96%)
  local copies, waits for them, and re-layouts  4.9 us (4%)
    pallas_call x1, Pallas kernels, per_device(): pl.pallas_call(kernel, out_shape=jax.ShapeDtypeStruct((K, I, C), BF16), i...  131 us
    transpose x1, local copies, waits for them, and re-layouts, per_device(): return jnp.transpose(result, (1, 0, 2))  4.9 us

profile of v4, /device:TPU:1, one launch (start us, length us, event | category | flops | bytes accessed | tf_op | source)
XLA Modules:
  0.0 135.6 jit_solution(14638141875884921244)
XLA Ops:
  0.0 130.7 %shard_map.82 = bf16[80,160,128]{2,1,0:T(8,128)(2,1)} custom-call(bf16[160,80,128]{2,1,0:T(8,128)(2,1)} %x_hbm.1, s32[160,80]{1,0:T(8,128)} %mask_ref.1, f32[1,128]{1,0:T(1,128)} %bitcast.6, f32[1,128]{1,0:T(1,128)} %bitcast.7, bf16[128,640]{1,0:T(8,128)(2,1)} %weights_ref.1, f32[1,128]{1,0:T(1,128)} %bitcast.8, f32[1,128]{1,0:T(1,128)} %bitcast.9, ...), custom_call_target="tpu_custom_call" | custom-call | flops 6499999744 | bytes 16000000 | tf_op jit(solution)/shard_map/pallas_call | solution.py:511
  130.7 4.9 %copy.9 = bf16[160,80,128]{2,1,0:T(8,128)(2,1)} copy(bf16[160,80,128]{2,0,1:T(8,128)(2,1)} %bitcast.5) | data formatting | bytes 6553600 | tf_op jit(solution)/shard_map/transpose | solution.py:563

commit v5 on v4

--- a/solution.py
+++ b/solution.py
@@ -16,10 +16,11 @@
 G = 16
 A = 8
 N = 1280
+PIECES = 8
 REST = 24
 BOTH = 40
-FIRST = 64
-R_MAIN, BOTH_REST, L_MAIN, T_REST, T_FIRST, T_LAST = range(6)
+FIRST = 48
+R_MAIN, BOTH_REST, L_MAIN, T_REST, T_FIRST, T_NEXT, T_LAST = range(7)
 
 
 def kernel(
@@ -34,6 +35,7 @@
     o_hbm,
     x_ref,
     o_ref,
+    late,
     wide,
     normed,
     gates,
@@ -160,13 +162,13 @@
             )
             return carry
 
-        lax.fori_loop(0, I // 32, rows, 0)
+        lax.fori_loop(0, I // 32, rows, 0, unroll=5)
 
         def turn(k, carry):
             normed[b * 16 + k] = wide[pl.ds(k, I, stride=16), :].astype(BF16)
             return carry
 
-        lax.fori_loop(0, 16, turn, 0, unroll=2)
+        lax.fori_loop(0, 16, turn, 0, unroll=8)
 
     def gated(tokens, weights, mask_rows):
         both = lax.dot_general(
@@ -241,7 +243,7 @@
             project_main(start + p * 2, p * 2, first)
             return carry
 
-        lax.fori_loop(0, count // 2, pair, 0)
+        lax.fori_loop(0, count // 2, pair, 0, unroll=4)
 
     def left_rows(start, count):
         project_rows(start, count, 0)
@@ -250,35 +252,41 @@
     def right_rows(start, count):
         project_rows(start, count, 2 * C)
         send_main(start, count, out_r, in_r, R_MAIN)
+
+    def normalize_two(b):
+        for n in (b, b + 1):
+            fetch(n).wait()
+            normalize(n)
 
     fetch(0).wait()
     normalize(0)
     pl.semaphore_wait(barrier, G + A - 2)
     greet_row(entry_sem)
-    project_rows(0, 16, 2 * C)
+    fetch(1).wait()
+    normalize(1)
+    project_rows(0, 32, 2 * C)
     pl.semaphore_wait(entry_sem, A - 1)
-    send_main(0, 16, out_r, in_r, R_MAIN)
-    left_rows(0, 16)
-    for b in range(2):
-        fetch(2 * b + 1).wait()
-        normalize(2 * b + 1)
-        fetch(2 * b + 2).wait()
-        normalize(2 * b + 2)
-        right_rows(32 * b + 16, 32)
+    send_main(0, 32, out_r, in_r, R_MAIN)
+    left_rows(0, 32)
+    normalize_two(2)
+    right_rows(32, 32)
+    fetch(4).wait()
+    normalize(4)
+    right_rows(64, 16)
 
     def low_rest(p, carry):
         project_rest(p * 2, p * 2, True, 2 * C)
         project_rest(p * 2, 16 + p * 2, True, 0)
         return carry
 
-    lax.fori_loop(0, 8, low_rest, 0)
+    lax.fori_loop(0, 8, low_rest, 0, unroll=2)
 
     def high_rest(p, carry):
         project_rest(p * 2, 32 + p * 2, False, 2 * C)
         project_rest(p * 2, 36 + p * 2, False, 0)
         return carry
 
-    lax.fori_loop(0, 2, high_rest, 0)
+    lax.fori_loop(0, 2, high_rest, 0, unroll=2)
 
     def prepare_rest(c):
         out_rest[c] = swap[pl.ds(c, BOTH, stride=C), :].astype(BF16)
@@ -287,8 +295,8 @@
         prepare_rest, lambda pg, pa: out_rest.at[pg * A + pa], in_rest.at[a, g], BOTH_REST
     )
 
-    left_rows(16, 32)
-    left_rows(48, 32)
+    left_rows(32, 32)
+    left_rows(64, 16)
 
     def open_gate(p, carry):
         tokens = normed[pl.ds(p * 2, 2)].reshape(2 * I, C)
@@ -296,7 +304,7 @@
         gates[pl.ds(p * 2, 2)] = (0.5 + 0.5 * jnp.tanh(half)).reshape(2, I, C)
         return carry
 
-    lax.fori_loop(0, K // 2, open_gate, 0)
+    lax.fori_loop(0, K // 2, open_gate, 0, unroll=4)
 
     def spread_rest(side, rest):
         def one(step, carry):
@@ -328,7 +336,7 @@
             rest[h, pl.ds(by_16(at + 64), 16), :] = joined.astype(BF16)
             return carry
 
-        lax.fori_loop(0, 2 * G, one, 0)
+        lax.fori_loop(0, 2 * G, one, 0, unroll=2)
 
     wait_all(in_r, recv_sem.at[R_MAIN])
 
@@ -425,8 +433,9 @@
         return carry
 
     lax.fori_loop(0, 16, main_product, 0)
-    last = pl.ds(FIRST, K - FIRST)
-    send_round(ready, lambda pg, pa: out_t.at[pg, pa, last], in_t.at[mine, last], T_LAST)
+    later = ((T_NEXT, pl.ds(FIRST, 16)), (T_LAST, pl.ds(FIRST + 16, 16)))
+    for which, rows in later:
+        send_round(ready, lambda pg, pa: out_t.at[pg, pa, rows], in_t.at[mine, rows], which)
 
     def settle(r, rows):
         values = swap[pl.ds(r, C, stride=rows), :]
@@ -445,17 +454,23 @@
             ].astype(F32)
             return carry
 
-        lax.fori_loop(0, C, one, 0, unroll=8)
+        lax.fori_loop(0, C, one, 0, unroll=16)
 
     def finish(b, carry):
         widen(in_t, by_16(b * 16), 16)
 
         def one(r, carry):
-            j = b * 16 + r
-            o_ref[j, 0:128, :] = (gates[j, 0:128, :] * settle(r, 16)).astype(BF16)
-            return carry
-
-        lax.fori_loop(0, 16, one, 0, unroll=4)
+            mixed = settle(r, 16)
+            wide[pl.ds(pl.multiple_of(r * 128, 128), 128), :] = gates[b * 16 + r, 0:128, :] * mixed
+            return carry
+
+        lax.fori_loop(0, 16, one, 0, unroll=16)
+
+        def turn(i, carry):
+            o_ref[i, pl.ds(by_16(b * 16), 16), :] = wide[pl.ds(i, 16, stride=128), :].astype(BF16)
+            return carry
+
+        lax.fori_loop(0, 128, turn, 0, unroll=16)
         return carry
 
     wait_all(in_t_rest, recv_sem.at[T_REST])
@@ -466,23 +481,36 @@
             mixed = settle(r, rows)
             for s in range(4):
                 j = token(s, r, low)
-                o_ref[j, 128:, :] = (
+                late[pl.ds(pl.multiple_of(j * 32, 32), 32), :] = (
                     gates[j, 128:, :] * mixed[32 * s : 32 * s + 32]
-                ).astype(BF16)
+                )
             return carry
 
         lax.fori_loop(0, count, one_rest, 0, unroll=4)
+
+    def turn_late(step, carry):
+        b, i = step >> 5, step & 31
+        o_ref[128 + i, pl.ds(by_16(b * 16), 16), :] = late[
+            pl.ds(b * 512 + i, 16, stride=32), :
+        ].astype(BF16)
+        return carry
+
+    lax.fori_loop(0, 160, turn_late, 0, unroll=8)
 
     wait_all(in_t.at[:, pl.ds(0, FIRST)], recv_sem.at[T_FIRST])
     lax.fori_loop(0, FIRST // 16, finish, 0)
 
     def put(number, block):
-        return pltpu.make_async_copy(o_ref.at[block], o_hbm.at[block], store_sem.at[number])
-
-    put(0, pl.ds(0, FIRST)).start()
-    wait_all(in_t.at[:, last], recv_sem.at[T_LAST])
-    lax.fori_loop(FIRST // 16, K // 16, finish, 0)
-    put(1, last).start()
+        return pltpu.make_async_copy(
+            o_ref.at[:, block], o_hbm.at[:, block], store_sem.at[number]
+        )
+
+    blocks = (pl.ds(0, FIRST),) + tuple(rows for _, rows in later)
+    put(0, blocks[0]).start()
+    for n, (which, rows) in enumerate(later):
+        wait_all(in_t.at[:, rows], recv_sem.at[which])
+        finish(FIRST // 16 + n, 0)
+        put(n + 1, blocks[n + 1]).start()
 
     for which, buffer in (
         (R_MAIN, out_r),
@@ -490,11 +518,30 @@
         (L_MAIN, out_l),
         (T_REST, in_t_rest),
         (T_FIRST, in_t.at[:, pl.ds(0, FIRST)]),
-        (T_LAST, in_t.at[:, last]),
+        *((which, in_t.at[:, rows]) for which, rows in later),
     ):
         wait_all(buffer.at[pl.ds(0, 127)], send_sem.at[which])
-    put(0, pl.ds(0, FIRST)).wait()
-    put(1, last).wait()
+    for n, block in enumerate(blocks):
+        put(n, block).wait()
+
+
+def store(from_ref, to_ref, held, sem):
+    pieces = [pl.ds(n * (I // PIECES), I // PIECES) for n in range(PIECES)]
+    arrive = [
+        pltpu.make_async_copy(from_ref.at[piece], held.at[piece], sem.at[n])
+        for n, piece in enumerate(pieces)
+    ]
+    leave = [
+        pltpu.make_async_copy(held.at[piece], to_ref.at[piece], sem.at[n])
+        for n, piece in enumerate(pieces)
+    ]
+    for copy in arrive:
+        copy.start()
+    for first, second in zip(arrive, leave):
+        first.wait()
+        second.start()
+    for copy in leave:
+        copy.wait()
 
 
 def per_device(
@@ -510,12 +557,13 @@
     vmem = pl.BlockSpec(memory_space=pltpu.VMEM)
     result = pl.pallas_call(
         kernel,
-        out_shape=jax.ShapeDtypeStruct((K, I, C), BF16),
+        out_shape=jax.ShapeDtypeStruct((I, K, C), BF16),
         in_specs=[pl.BlockSpec(memory_space=pl.ANY)] + [vmem] * 7,
         out_specs=pl.BlockSpec(memory_space=pl.ANY),
         scratch_shapes=[
             pltpu.VMEM((I, K, C), BF16),
-            pltpu.VMEM((K, I, C), BF16),
+            pltpu.VMEM((I, K, C), BF16),
+            pltpu.VMEM((K * 32, C), F32),
             pltpu.VMEM((I * 16, C), F32),
             pltpu.VMEM((K, I, C), BF16),
             pltpu.VMEM((K, I, C), F32),
@@ -539,10 +587,10 @@
             pltpu.VMEM((2, N, 128), BF16),
             pltpu.VMEM((N, N), BF16),
             pltpu.SemaphoreType.DMA((5,)),
-            pltpu.SemaphoreType.DMA((2,)),
+            pltpu.SemaphoreType.DMA((3,)),
             pltpu.SemaphoreType.REGULAR,
-            pltpu.SemaphoreType.DMA((6,)),
-            pltpu.SemaphoreType.DMA((6,)),
+            pltpu.SemaphoreType.DMA((7,)),
+            pltpu.SemaphoreType.DMA((7,)),
         ],
         compiler_params=pltpu.CompilerParams(
             collective_id=0, has_side_effects=True, vmem_limit_bytes=58 * 2**20
@@ -560,7 +608,16 @@
         output_bias[None],
         output_weight,
     )
-    return jnp.transpose(result, (1, 0, 2))
+    anywhere = pl.BlockSpec(memory_space=pl.ANY)
+    return pl.pallas_call(
+        store,
+        out_shape=jax.ShapeDtypeStruct((I, K, C), BF16),
+        in_specs=[anywhere],
+        out_specs=anywhere,
+        scratch_shapes=[pltpu.VMEM((I, K, C), BF16), pltpu.SemaphoreType.DMA((PIECES,))],
+        compiler_params=pltpu.CompilerParams(vmem_limit_bytes=58 * 2**20),
+        cost_estimate=pl.CostEstimate(flops=0, bytes_accessed=6_600_000, transcendentals=0),
+    )(result)
 
 
 def solution(mesh):

time: 136 us -> 130 us (0.956)
  local copies, waits for them, and re-layouts: 4.9 us -> 0 us
  Pallas kernels: 131 us -> 129 us
    transpose x1 -> x0, local copies, waits for them, and re-layouts: 4.9 us -> none  [per_device(): return jnp.transpose(result, (1, 0, 2))]
    pallas_call x1 -> x2, Pallas kernels: 131 us -> 129 us  [the longest x1 127 us: per_device(): pl.pallas_call(kernel, out_shape=jax.ShapeDtypeStruct((I, K, C), BF16), i...]
where the time goes in v5:
time: 130 us; the launch traced here: 129 us
  Pallas kernels  129 us (99%)
    pallas_call x1, Pallas kernels, per_device(): pl.pallas_call(kernel, out_shape=jax.ShapeDtypeStruct((I, K, C), BF16), i...  127 us
    pallas_call x1, Pallas kernels, per_device(): pl.pallas_call(store, out_shape=jax.ShapeDtypeStruct((I, K, C), BF16), in...  2.77 us

profile of v5, /device:TPU:1, one launch (start us, length us, event | category | flops | bytes accessed | tf_op | source)
XLA Modules:
  0.0 129.4 jit_solution(4004766325491349344)
XLA Ops:
  0.0 126.6 %shard_map.82.from_ref = bf16[160,80,128]{2,1,0:T(8,128)(2,1)} custom-call(bf16[160,80,128]{2,1,0:T(8,128)(2,1)} %x_hbm.1, s32[160,80]{1,0:T(8,128)} %mask_ref.1, f32[1,128]{1,0:T(1,128)} %bitcast.4, f32[1,128]{1,0:T(1,128)} %bitcast.5, bf16[128,640]{1,0:T(8,128)(2,1)} %weights_ref.1, f32[1,128]{1,0:T(1,128)} %bitcast.6, f32[1,128]{1,0:T(1,128)} %bitcast.7, ...), custom_call_target="tpu_custom_call" | custom-call | flops 6499999744 | bytes 16000000 | tf_op jit(solution)/shard_map/pallas_call | solution.py:558
  126.6 2.8 %shard_map.83 = bf16[160,80,128]{2,1,0:T(8,128)(2,1)} custom-call(bf16[160,80,128]{2,1,0:T(8,128)(2,1)} %shard_map.82.from_ref), custom_call_target="tpu_custom_call" | custom-call | bytes 6600000 | tf_op jit(solution)/shard_map/pallas_call | solution.py:612

commit v6 on v5

--- a/solution.py
+++ b/solution.py
@@ -16,7 +16,6 @@
 G = 16
 A = 8
 N = 1280
-PIECES = 8
 REST = 24
 BOTH = 40
 FIRST = 48
@@ -32,9 +31,8 @@
     ogain_ref,
     obias_ref,
     ow_ref,
-    o_hbm,
+    o_ref,
     x_ref,
-    o_ref,
     late,
     wide,
     normed,
@@ -59,7 +57,6 @@
     rest_r,
     right_t,
     fetch_sem,
-    store_sem,
     entry_sem,
     send_sem,
     recv_sem,
@@ -95,6 +92,13 @@
         lax.fori_loop(0, 18, several, 0)
         visit(*partner(127))
 
+    def fetch(b):
+        block = pl.ds(b * 16, 16)
+        return pltpu.make_async_copy(x_hbm.at[:, block], x_ref.at[:, block], fetch_sem.at[b])
+
+    for b in range(5):
+        fetch(b).start()
+
     def greet_row(semaphore):
         for step in range(1, A):
             pl.semaphore_signal(
@@ -112,13 +116,6 @@
 
     lax.fori_loop(1, G, greet_column, 0, unroll=5)
     greet_row(barrier)
-
-    def fetch(b):
-        block = pl.ds(b * 16, 16)
-        return pltpu.make_async_copy(x_hbm.at[:, block], x_ref.at[:, block], fetch_sem.at[b])
-
-    for b in range(5):
-        fetch(b).start()
 
     def by_group(parts):
         group = lax.broadcasted_iota(jnp.int32, parts[0].shape, 1) // 32
@@ -262,17 +259,13 @@
     normalize(0)
     pl.semaphore_wait(barrier, G + A - 2)
     greet_row(entry_sem)
-    fetch(1).wait()
-    normalize(1)
-    project_rows(0, 32, 2 * C)
+    project_rows(0, 16, 2 * C)
     pl.semaphore_wait(entry_sem, A - 1)
-    send_main(0, 32, out_r, in_r, R_MAIN)
-    left_rows(0, 32)
-    normalize_two(2)
-    right_rows(32, 32)
-    fetch(4).wait()
-    normalize(4)
-    right_rows(64, 16)
+    send_main(0, 16, out_r, in_r, R_MAIN)
+    left_rows(0, 16)
+    for b in range(2):
+        normalize_two(2 * b + 1)
+        right_rows(32 * b + 16, 32)
 
     def low_rest(p, carry):
         project_rest(p * 2, p * 2, True, 2 * C)
@@ -295,8 +288,8 @@
         prepare_rest, lambda pg, pa: out_rest.at[pg * A + pa], in_rest.at[a, g], BOTH_REST
     )
 
-    left_rows(32, 32)
-    left_rows(64, 16)
+    left_rows(16, 32)
+    left_rows(48, 32)
 
     def open_gate(p, carry):
         tokens = normed[pl.ds(p * 2, 2)].reshape(2 * I, C)
@@ -499,18 +492,9 @@
 
     wait_all(in_t.at[:, pl.ds(0, FIRST)], recv_sem.at[T_FIRST])
     lax.fori_loop(0, FIRST // 16, finish, 0)
-
-    def put(number, block):
-        return pltpu.make_async_copy(
-            o_ref.at[:, block], o_hbm.at[:, block], store_sem.at[number]
-        )
-
-    blocks = (pl.ds(0, FIRST),) + tuple(rows for _, rows in later)
-    put(0, blocks[0]).start()
     for n, (which, rows) in enumerate(later):
         wait_all(in_t.at[:, rows], recv_sem.at[which])
         finish(FIRST // 16 + n, 0)
-        put(n + 1, blocks[n + 1]).start()
 
     for which, buffer in (
         (R_MAIN, out_r),
@@ -521,27 +505,6 @@
         *((which, in_t.at[:, rows]) for which, rows in later),
     ):
         wait_all(buffer.at[pl.ds(0, 127)], send_sem.at[which])
-    for n, block in enumerate(blocks):
-        put(n, block).wait()
-
-
-def store(from_ref, to_ref, held, sem):
-    pieces = [pl.ds(n * (I // PIECES), I // PIECES) for n in range(PIECES)]
-    arrive = [
-        pltpu.make_async_copy(from_ref.at[piece], held.at[piece], sem.at[n])
-        for n, piece in enumerate(pieces)
-    ]
-    leave = [
-        pltpu.make_async_copy(held.at[piece], to_ref.at[piece], sem.at[n])
-        for n, piece in enumerate(pieces)
-    ]
-    for copy in arrive:
-        copy.start()
-    for first, second in zip(arrive, leave):
-        first.wait()
-        second.start()
-    for copy in leave:
-        copy.wait()
 
 
 def per_device(
@@ -557,11 +520,10 @@
     vmem = pl.BlockSpec(memory_space=pltpu.VMEM)
     result = pl.pallas_call(
         kernel,
-        out_shape=jax.ShapeDtypeStruct((I, K, C), BF16),
+        out_shape=pltpu.VMEM((I, K, C), BF16),
         in_specs=[pl.BlockSpec(memory_space=pl.ANY)] + [vmem] * 7,
-        out_specs=pl.BlockSpec(memory_space=pl.ANY),
+        out_specs=vmem,
         scratch_shapes=[
-            pltpu.VMEM((I, K, C), BF16),
             pltpu.VMEM((I, K, C), BF16),
             pltpu.VMEM((K * 32, C), F32),
             pltpu.VMEM((I * 16, C), F32),
@@ -587,7 +549,6 @@
             pltpu.VMEM((2, N, 128), BF16),
             pltpu.VMEM((N, N), BF16),
             pltpu.SemaphoreType.DMA((5,)),
-            pltpu.SemaphoreType.DMA((3,)),
             pltpu.SemaphoreType.REGULAR,
             pltpu.SemaphoreType.DMA((7,)),
             pltpu.SemaphoreType.DMA((7,)),
@@ -608,16 +569,7 @@
         output_bias[None],
         output_weight,
     )
-    anywhere = pl.BlockSpec(memory_space=pl.ANY)
-    return pl.pallas_call(
-        store,
-        out_shape=jax.ShapeDtypeStruct((I, K, C), BF16),
-        in_specs=[anywhere],
-        out_specs=anywhere,
-        scratch_shapes=[pltpu.VMEM((I, K, C), BF16), pltpu.SemaphoreType.DMA((PIECES,))],
-        compiler_params=pltpu.CompilerParams(vmem_limit_bytes=58 * 2**20),
-        cost_estimate=pl.CostEstimate(flops=0, bytes_accessed=6_600_000, transcendentals=0),
-    )(result)
+    return result
 
 
 def solution(mesh):

time: 130 us -> 127 us (0.977)
  Pallas kernels: 129 us -> 125 us
  local copies, waits for them, and re-layouts: 0 us -> 1.71 us
    pallas_call x2 -> x1, Pallas kernels: 129 us -> 125 us  [per_device(): pl.pallas_call(kernel, out_shape=pltpu.VMEM((I, K, C), BF16), in_specs=[p...]
    unnamed x0 -> x1, local copies, waits for them, and re-layouts: none -> 1.71 us
where the time goes in v6:
time: 127 us
  Pallas kernels  125 us (98%)
  local copies, waits for them, and re-layouts  1.71 us (1%)
    pallas_call x1, Pallas kernels, per_device(): pl.pallas_call(kernel, out_shape=pltpu.VMEM((I, K, C), BF16), in_specs=[p...  125 us

profile of v6, /device:TPU:1, one launch (start us, length us, event | category | flops | bytes accessed | tf_op | source)
XLA Modules:
  0.0 127.1 jit_solution(3887124895844113720)
XLA Ops:
  0.0 125.4 %shard_map.82 = bf16[160,80,128]{2,1,0:T(8,128)(2,1)S(1)} custom-call(bf16[160,80,128]{2,1,0:T(8,128)(2,1)} %x_hbm.1, s32[160,80]{1,0:T(8,128)} %mask_ref.1, f32[1,128]{1,0:T(1,128)} %bitcast.4, f32[1,128]{1,0:T(1,128)} %bitcast.5, bf16[128,640]{1,0:T(8,128)(2,1)} %weights_ref.1, f32[1,128]{1,0:T(1,128)} %bitcast.6, f32[1,128]{1,0:T(1,128)} %bitcast.7, ...), custom_call_target="tpu_custom_call" | custom-call | flops 6499999744 | bytes 16000000 | tf_op jit(solution)/shard_map/pallas_call | solution.py:521
  125.4 1.7 %copy.10 = bf16[160,80,128]{2,1,0:T(8,128)(2,1)} copy(bf16[160,80,128]{2,1,0:T(8,128)(2,1)S(1)} %shard_map.82) | data formatting | bytes 6553600

commit v7 on v6

--- a/solution.py
+++ b/solution.py
@@ -24,6 +24,15 @@
 
 def kernel(
     x_hbm,
+    mask_hbm,
+    gain_hbm,
+    bias_hbm,
+    weights_hbm,
+    ogain_hbm,
+    obias_hbm,
+    ow_hbm,
+    o_ref,
+    x_ref,
     mask_ref,
     gain_ref,
     bias_ref,
@@ -31,8 +40,6 @@
     ogain_ref,
     obias_ref,
     ow_ref,
-    o_ref,
-    x_ref,
     late,
     wide,
     normed,
@@ -57,6 +64,7 @@
     rest_r,
     right_t,
     fetch_sem,
+    small_sem,
     entry_sem,
     send_sem,
     recv_sem,
@@ -92,12 +100,29 @@
         lax.fori_loop(0, 18, several, 0)
         visit(*partner(127))
 
+    smalls = [
+        pltpu.make_async_copy(source, target, small_sem.at[n])
+        for n, (source, target) in enumerate(
+            (
+                (weights_hbm, weights_ref),
+                (mask_hbm, mask_ref),
+                (gain_hbm, gain_ref),
+                (bias_hbm, bias_ref),
+                (ogain_hbm, ogain_ref),
+                (obias_hbm, obias_ref),
+                (ow_hbm, ow_ref),
+            )
+        )
+    ]
+
     def fetch(b):
         block = pl.ds(b * 16, 16)
         return pltpu.make_async_copy(x_hbm.at[:, block], x_ref.at[:, block], fetch_sem.at[b])
 
     for b in range(5):
         fetch(b).start()
+    for copy in smalls:
+        copy.start()
 
     def greet_row(semaphore):
         for step in range(1, A):
@@ -131,6 +156,9 @@
 
     def by_16(value):
         return pl.multiple_of(value, 16)
+
+    for copy in smalls:
+        copy.wait()
 
     for part in range(4):
         columns = weights_ref[:, part * C : (part + 1) * C].astype(F32)
@@ -521,10 +549,17 @@
     result = pl.pallas_call(
         kernel,
         out_shape=pltpu.VMEM((I, K, C), BF16),
-        in_specs=[pl.BlockSpec(memory_space=pl.ANY)] + [vmem] * 7,
+        in_specs=[pl.BlockSpec(memory_space=pl.ANY)] * 8,
         out_specs=vmem,
         scratch_shapes=[
             pltpu.VMEM((I, K, C), BF16),
+            pltpu.VMEM((I, K), jnp.int32),
+            pltpu.VMEM((1, C), F32),
+            pltpu.VMEM((1, C), F32),
+            pltpu.VMEM((C, 5 * C), BF16),
+            pltpu.VMEM((1, C), F32),
+            pltpu.VMEM((1, C), F32),
+            pltpu.VMEM((C, C), BF16),
             pltpu.VMEM((K * 32, C), F32),
             pltpu.VMEM((I * 16, C), F32),
             pltpu.VMEM((K, I, C), BF16),
@@ -549,6 +584,7 @@
             pltpu.VMEM((2, N, 128), BF16),
             pltpu.VMEM((N, N), BF16),
             pltpu.SemaphoreType.DMA((5,)),
+            pltpu.SemaphoreType.DMA((7,)),
             pltpu.SemaphoreType.REGULAR,
             pltpu.SemaphoreType.DMA((7,)),
             pltpu.SemaphoreType.DMA((7,)),

time: 127 us -> 126 us (level)
  no operation moved by 1% of the time
where the time goes in v7:
time: 126 us
  Pallas kernels  125 us (99%)
  local copies, waits for them, and re-layouts  1.71 us (1%)
    pallas_call x1, Pallas kernels, per_device(): pl.pallas_call(kernel, out_shape=pltpu.VMEM((I, K, C), BF16), in_specs=[p...  125 us

profile of v7, /device:TPU:1, one launch (start us, length us, event | category | flops | bytes accessed | tf_op | source)
XLA Modules:
  0.0 126.4 jit_solution(748280769351338289)
XLA Ops:
  0.0 124.7 %shard_map.82 = bf16[160,80,128]{2,1,0:T(8,128)(2,1)S(1)} custom-call(bf16[160,80,128]{2,1,0:T(8,128)(2,1)} %x_hbm.1, s32[160,80]{1,0:T(8,128)} %mask_hbm.1, f32[1,128]{1,0:T(1,128)} %bitcast.4, f32[1,128]{1,0:T(1,128)} %bitcast.5, bf16[128,640]{1,0:T(8,128)(2,1)} %weights_hbm.1, f32[1,128]{1,0:T(1,128)} %bitcast.6, f32[1,128]{1,0:T(1,128)} %bitcast.7, ...), custom_call_target="tpu_custom_call" | custom-call | flops 6499999744 | bytes 16000000 | tf_op jit(solution)/shard_map/pallas_call | solution.py:549
  124.7 1.7 %copy.10 = bf16[160,80,128]{2,1,0:T(8,128)(2,1)} copy(bf16[160,80,128]{2,1,0:T(8,128)(2,1)S(1)} %shard_map.82) | data formatting | bytes 6553600
